TPU v7x, 512 devices: a whole 4x8x8 slice. The times are simulated.
512 devices in a mesh: win: 64 (over y, x, core), pair: 8 (over z).
Axes of the slice: x: 4, y: 8, z: 8, core: 2. Of those that a mesh axis runs over, the one named last changes fastest.
Arguments:
- spectra: float32 [128, 8, 64, 4096], P('win', 'pair'), may hold values from -6 to 6
- counts: int32 [64, 8], P('win', 'pair'), may hold values from 1 to 2
- band_filter: float32 [2048], replicated, may hold values from 0.1 to 1
- pair_list: int32 [8, 6, 2], P('pair'), may hold values from 0 to 7, as said below
- live_slots: int32 [8], P('pair'), may hold values from 1 to 6, as said below
Outputs:
- correlations: float32 [2048, 3072], P('win', 'pair')
Inputs may be any that keep to these rules, and one draw needn't show every extreme that they name: `pair_list`: slot entries (a, b) of owner p satisfy a <= b, p - 1 <= a and b <= p + 1. `live_slots`: some owner uses all 6 slots.
All inputs are finite; a program needn't handle non-finite values.
Results may differ from a plain program's by a relative error of at most 0.0011.
Values sent between devices are 32-bit elements; how exact they have to be, the bound alone decides.
A program may use at most 64 MiB of HBM per device.

v0:
```python
import math

import jax
import jax.numpy as jnp
from jax import lax
from jax.sharding import PartitionSpec as P

LAGS = 2048


def padded(block, sides, width):
    for axis, dim in sides:
        count = lax.axis_size(axis)
        forward = [(i, i + 1) for i in range(count - 1)]
        backward = [(target, source) for source, target in forward]
        low = lax.ppermute(
            lax.slice_in_dim(block, block.shape[dim] - width, None, axis=dim), axis, forward
        )
        high = lax.ppermute(lax.slice_in_dim(block, 0, width, axis=dim), axis, backward)
        block = jnp.concatenate([low, block, high], axis=dim)
    return block


def on_device(spectra, counts, band_filter, pair_list, live_slots):
    bin_count = band_filter.shape[0]
    channels = spectra.shape[2]
    whitened = spectra * lax.rsqrt(jnp.mean(spectra * spectra, axis=-1, keepdims=True) + 1e-06)
    extended, near_counts = (
        padded(whitened, (("pair", 1),), 1),
        padded(counts.astype(jnp.float32), (("pair", 1),), 1),
    )
    anchor = lax.axis_index("pair") - 1
    slot_table = pair_list[0]
    slot_total = slot_table.shape[0]
    first_local = slot_table[:, 0] - anchor
    second_local = slot_table[:, 1] - anchor
    weight = jnp.concatenate([band_filter, band_filter])
    windows = jnp.arange(spectra.shape[0], dtype=jnp.float32)
    live_now = live_slots[0]

    def one_slot(slot_item):
        left_index, right_index, slot_index = slot_item
        left_spec = lax.dynamic_index_in_dim(extended, left_index, 1, keepdims=False)
        right_spec = lax.dynamic_index_in_dim(extended, right_index, 1, keepdims=False)
        kept_count = jnp.minimum(near_counts[0, left_index], near_counts[0, right_index])
        window_mask = (windows < kept_count).astype(jnp.float32)[:, None, None]
        left_real, left_imag = (left_spec[..., :bin_count], left_spec[..., bin_count:])
        right_real, right_imag = (right_spec[..., :bin_count], right_spec[..., bin_count:])
        real_part = jnp.sum(window_mask * (left_real * right_real + left_imag * right_imag), axis=0)
        imag_part = jnp.sum(window_mask * (left_imag * right_real - left_real * right_imag), axis=0)
        alive_flag = (slot_index < live_now).astype(jnp.float32)
        stacked = (jnp.concatenate([real_part, imag_part], axis=-1) * weight * alive_flag).astype(
            jnp.bfloat16
        )
        return (stacked, kept_count)

    stacked, kept_counts = lax.map(
        one_slot, (first_local, second_local, jnp.arange(slot_total, dtype=jnp.int32))
    )
    stack_rows = stacked.reshape(slot_total * channels, 2 * bin_count)
    totals = lax.psum(kept_counts, "win")
    column_scale = jnp.repeat(1.0 / totals, channels)
    lag_share = LAGS // lax.axis_size("win")
    block_rows = math.gcd(LAGS, 256)
    columns = jnp.arange(2 * bin_count, dtype=jnp.int32)
    frequency = columns % bin_count

    def one_block(block_index):
        lag_values = (
            0 + block_index * block_rows + jnp.arange(block_rows, dtype=jnp.int32) - LAGS // 2
        )
        phase_angle = jnp.mod(lag_values[:, None] * frequency[None, :], 2 * bin_count).astype(
            jnp.float32
        ) * (math.pi / bin_count)
        lag_table = jnp.where(
            columns[None, :] < bin_count, jnp.cos(phase_angle), -jnp.sin(phase_angle)
        ) * math.sqrt(2.0 / bin_count)
        lag_table = lag_table.astype(jnp.bfloat16)
        return lax.dot_general(
            lag_table, stack_rows, (((1,), (1,)), ((), ())), preferred_element_type=jnp.float32
        )

    pieces = lax.map(one_block, jnp.arange(LAGS // block_rows, dtype=jnp.int32))
    whole_term = lax.psum(pieces.reshape(LAGS, stack_rows.shape[0]), "win")
    summed = lax.dynamic_slice_in_dim(whole_term, lax.axis_index("win") * lag_share, lag_share, 0)
    return summed * column_scale[None, :]


def solution(mesh):
    placed = (P("win", "pair", None, None), P("win", "pair"), P(), P("pair", None, None), P("pair"))
    return jax.shard_map(
        on_device, mesh=mesh, in_specs=placed, out_specs=P("win", "pair"), check_vma=False
    )
```

profile of v0, /device:TPU:1, one launch (start us, length us, event | category | flops | bytes accessed | tf_op | source)
XLA Modules:
  0.0 540.3 jit_solution(7883091839246653468)
XLA Ops:
  6.5 2.0 multiply_reduce_fusion.2
  8.8 1.6 broadcast_multiply_fusion
  10.3 4.9 collective-permute-start.2
  15.3 1.3 collective-permute-start.3
  17.3 40.1 %collective-permute-start = (f32[1,1]{1,0:T(1,128)}, f32[1,1]{1,0:T(1,128)}, u32[]{:S(2)}, u32[]{:S(2)}) collective-permute-start(f32[1,1]{1,0:T(1,128)} %convert_element_type.35), channel_id=1, source_target_pairs={{0,1},{1,2},{2,3},{3,4},{4,5},{5,6},{6,7},{8,9},{9,10},{10,11},{11... | collective-permute-start | bytes 20 | tf_op jit(solution)/shard_map/ppermute | solution.py:16
  57.3 1.3 collective-permute-start.1
  58.7 6.4 %collective-permute-done.1 = f32[1,1]{1,0:T(1,128)} collective-permute-done((f32[1,1]{1,0:T(1,128)}, f32[1,1]{1,0:T(1,128)}, u32[]{:S(2)}, u32[]{:S(2)}) %collective-permute-start.1) | collective-permute-done | bytes 36 | tf_op jit(solution)/shard_map/ppermute | solution.py:19
  65.1 1.3 pad_maximum_fusion.2
  66.5 5.5 %pad_maximum_fusion = f32[2,3,64,4096]{3,2,1,0:T(8,128)} fusion(f32[2,1,64,4096]{3,2,1,0:T(8,128)} %collective-permute-done.3, f32[2,1,64,4096]{3,2,1,0:T(8,128)} %broadcast_multiply_fusion, f32[2,1,64,4096]{3,2,1,0:T(8,128)S(1)} %collective-permute-done.2), kind=kLoop, calls=%fused_computation.47 | loop fusion | flops 3145728 | bytes 12582912 | tf_op jit(solution)/shard_map/concatenate | solution.py:20
  72.0 78.8 %while.26 = (s32[]{:T(128)}, bf16[6,64,4096]{2,1,0:T(8,128)(2,1)}, f32[6]{0:T(128)S(1)}, s32[6]{0:T(128)S(1)}, f32[1,3]{1,0:T(1,128)S(1)}, /*index=5*/s32[6]{0:T...) while((s32[]{:T(128)}, bf16[6,64,4096]{2,1,0:T(8,128)(2,1)}, ...), condition=%wide.region_4.5_spmd.clone, body=%wide.region_1.4_spmd.clone.sunk | while | flops 3407887 | bytes 15221591 | solution.py:57
  72.0 0.6 dynamic_slice.56
  74.5 0.7 dynamic_slice.55
  77.0 2.6 dynamic-slice_bitcast_fusion.3
  79.6 0.7 constant_dynamic-slice_fusion.3
  82.2 0.7 dynamic_slice.57
  84.2 0.9 fusion.35
  85.1 0.7 dynamic_slice.56
  87.6 0.7 dynamic_slice.55
  90.1 2.5 dynamic-slice_bitcast_fusion.3
  92.7 0.7 constant_dynamic-slice_fusion.3
  95.3 0.7 dynamic_slice.57
  97.3 0.9 fusion.35
  98.2 0.7 dynamic_slice.56
  100.7 0.7 dynamic_slice.55
  103.2 2.6 dynamic-slice_bitcast_fusion.3
  105.8 0.7 constant_dynamic-slice_fusion.3
  108.4 0.7 dynamic_slice.57
  110.4 0.9 fusion.35
  111.4 0.7 dynamic_slice.56
  113.9 0.7 dynamic_slice.55
  116.4 2.6 dynamic-slice_bitcast_fusion.3
  119.0 0.7 constant_dynamic-slice_fusion.3
  121.6 0.7 dynamic_slice.57
  123.6 0.9 fusion.35
  124.5 0.7 dynamic_slice.56
  127.0 0.7 dynamic_slice.55
  129.5 2.6 dynamic-slice_bitcast_fusion.3
  132.1 0.7 constant_dynamic-slice_fusion.3
  134.7 0.7 dynamic_slice.57
  136.7 0.9 fusion.35
  137.6 0.7 dynamic_slice.56
  140.2 0.7 dynamic_slice.55
  142.7 2.6 dynamic-slice_bitcast_fusion.3
  145.2 0.7 constant_dynamic-slice_fusion.3
  147.8 0.7 dynamic_slice.57
  149.8 0.9 fusion.35
  150.8 174.8 %while.27 = (s32[]{:T(128)}, f32[8,256,384]{2,1,0:T(8,128)}, s32[8]{0:T(128)S(1)}, bf16[384,4096]{1,0:T(8,128)(2,1)}, s32[]{:T(128)}, /*index=5*/s32[1]{0:T(128)}) while((s32[]{:T(128)}, f32[8,256,384]{2,1,0:T(8,128)}, s32[8]{0:T(128)S(1)}, bf16[384,4096]{1,0:T(8,128)(2,1)}, s32[]{:T(128)}, /*index=5*/s32[1]{0:T(128)}) %tuple.63), condition=%wide.region_6.7_spmd.clone, body=%wide.region_5.6_spmd.clone.sunk | while | flops 824209920 | bytes 3582561 | solution.py:83
  151.0 0.6 dynamic_slice.58
  152.3 20.5 %fusion.37 = f32[8,256,384]{2,1,0:T(8,128)} fusion(f32[8,256,384]{2,1,0:T(8,128)} %get-tuple-element.358, s32[]{:T(128)} %get-tuple-element.357, bf16[384,4096]{1,0:T(8,128)(2,1)} %get-tuple-element.366, s32[4096]{0:T(1024)S(1)} %add_select_fusion.3, s32[256]{0:T(256)S(1)} %add_add_fusion.2, pred[4096]{0:T(1024)(128)(4,1)S(1)} %iota_compare_fusion.2), kind=kOutput, calls=%fused_computation.34.clone.1 | convolution fusion | flops 824180736 | bytes 3560960 | tf_op jit(solution)/shard_map/while/body/eval_jaxpr/dot_general | solution.py:79
  172.8 0.6 dynamic_slice.58
  174.1 20.5 %fusion.37 = f32[8,256,384]{2,1,0:T(8,128)} fusion(f32[8,256,384]{2,1,0:T(8,128)} %get-tuple-element.358, s32[]{:T(128)} %get-tuple-element.357, bf16[384,4096]{1,0:T(8,128)(2,1)} %get-tuple-element.366, s32[4096]{0:T(1024)S(1)} %add_select_fusion.3, s32[256]{0:T(256)S(1)} %add_add_fusion.2, pred[4096]{0:T(1024)(128)(4,1)S(1)} %iota_compare_fusion.2), kind=kOutput, calls=%fused_computation.34.clone.1 | convolution fusion | flops 824180736 | bytes 3560960 | tf_op jit(solution)/shard_map/while/body/eval_jaxpr/dot_general | solution.py:79
  194.6 0.6 dynamic_slice.58
  195.9 20.5 %fusion.37 = f32[8,256,384]{2,1,0:T(8,128)} fusion(f32[8,256,384]{2,1,0:T(8,128)} %get-tuple-element.358, s32[]{:T(128)} %get-tuple-element.357, bf16[384,4096]{1,0:T(8,128)(2,1)} %get-tuple-element.366, s32[4096]{0:T(1024)S(1)} %add_select_fusion.3, s32[256]{0:T(256)S(1)} %add_add_fusion.2, pred[4096]{0:T(1024)(128)(4,1)S(1)} %iota_compare_fusion.2), kind=kOutput, calls=%fused_computation.34.clone.1 | convolution fusion | flops 824180736 | bytes 3560960 | tf_op jit(solution)/shard_map/while/body/eval_jaxpr/dot_general | solution.py:79
  216.5 0.6 dynamic_slice.58
  217.8 20.5 %fusion.37 = f32[8,256,384]{2,1,0:T(8,128)} fusion(f32[8,256,384]{2,1,0:T(8,128)} %get-tuple-element.358, s32[]{:T(128)} %get-tuple-element.357, bf16[384,4096]{1,0:T(8,128)(2,1)} %get-tuple-element.366, s32[4096]{0:T(1024)S(1)} %add_select_fusion.3, s32[256]{0:T(256)S(1)} %add_add_fusion.2, pred[4096]{0:T(1024)(128)(4,1)S(1)} %iota_compare_fusion.2), kind=kOutput, calls=%fused_computation.34.clone.1 | convolution fusion | flops 824180736 | bytes 3560960 | tf_op jit(solution)/shard_map/while/body/eval_jaxpr/dot_general | solution.py:79
  238.3 0.6 dynamic_slice.58
  239.6 20.5 %fusion.37 = f32[8,256,384]{2,1,0:T(8,128)} fusion(f32[8,256,384]{2,1,0:T(8,128)} %get-tuple-element.358, s32[]{:T(128)} %get-tuple-element.357, bf16[384,4096]{1,0:T(8,128)(2,1)} %get-tuple-element.366, s32[4096]{0:T(1024)S(1)} %add_select_fusion.3, s32[256]{0:T(256)S(1)} %add_add_fusion.2, pred[4096]{0:T(1024)(128)(4,1)S(1)} %iota_compare_fusion.2), kind=kOutput, calls=%fused_computation.34.clone.1 | convolution fusion | flops 824180736 | bytes 3560960 | tf_op jit(solution)/shard_map/while/body/eval_jaxpr/dot_general | solution.py:79
  260.1 0.6 dynamic_slice.58
  261.4 20.6 %fusion.37 = f32[8,256,384]{2,1,0:T(8,128)} fusion(f32[8,256,384]{2,1,0:T(8,128)} %get-tuple-element.358, s32[]{:T(128)} %get-tuple-element.357, bf16[384,4096]{1,0:T(8,128)(2,1)} %get-tuple-element.366, s32[4096]{0:T(1024)S(1)} %add_select_fusion.3, s32[256]{0:T(256)S(1)} %add_add_fusion.2, pred[4096]{0:T(1024)(128)(4,1)S(1)} %iota_compare_fusion.2), kind=kOutput, calls=%fused_computation.34.clone.1 | convolution fusion | flops 824180736 | bytes 3560960 | tf_op jit(solution)/shard_map/while/body/eval_jaxpr/dot_general | solution.py:79
  283.2 20.5 %fusion.37 = f32[8,256,384]{2,1,0:T(8,128)} fusion(f32[8,256,384]{2,1,0:T(8,128)} %get-tuple-element.358, s32[]{:T(128)} %get-tuple-element.357, bf16[384,4096]{1,0:T(8,128)(2,1)} %get-tuple-element.366, s32[4096]{0:T(1024)S(1)} %add_select_fusion.3, s32[256]{0:T(256)S(1)} %add_add_fusion.2, pred[4096]{0:T(1024)(128)(4,1)S(1)} %iota_compare_fusion.2), kind=kOutput, calls=%fused_computation.34.clone.1 | convolution fusion | flops 824180736 | bytes 3560960 | tf_op jit(solution)/shard_map/while/body/eval_jaxpr/dot_general | solution.py:79
  305.1 20.6 %fusion.37 = f32[8,256,384]{2,1,0:T(8,128)} fusion(f32[8,256,384]{2,1,0:T(8,128)} %get-tuple-element.358, s32[]{:T(128)} %get-tuple-element.357, bf16[384,4096]{1,0:T(8,128)(2,1)} %get-tuple-element.366, s32[4096]{0:T(1024)S(1)} %add_select_fusion.3, s32[256]{0:T(256)S(1)} %add_add_fusion.2, pred[4096]{0:T(1024)(128)(4,1)S(1)} %iota_compare_fusion.2), kind=kOutput, calls=%fused_computation.34.clone.1 | convolution fusion | flops 824180736 | bytes 3560960 | tf_op jit(solution)/shard_map/while/body/eval_jaxpr/dot_general | solution.py:79
  325.6 126.2 %psum.15 = f32[6]{0:T(128)S(1)} all-reduce(f32[6]{0:T(128)S(1)} %get-tuple-element.144), channel_id=1, replica_groups=mesh['win'=64,'pair'=8] {'win'}, use_global_device_ids=true, to_apply=%region_8.9 | all-reduce | flops 6 | bytes 48 | tf_op jit(solution)/shard_map/psum | solution.py:61
  452.0 80.1 %all-reduce.2.cloned.1.call-done = f32[2048,384]{1,0:T(8,128)} async-done(((f32[2048,384]{1,0:T(8,128)}), f32[2048,384]{1,0:T(8,128)}) %all-reduce.2.cloned.1.call-update) | async-done | bytes 3145744 | tf_op jit(solution)/shard_map/psum | solution.py:84
  532.0 1.4 dynamic-slice_multiply_fusion
  (66 shorter events, 5.4 us)
Async XLA Ops:
  6.5 2.2 copy-start
  6.5 52.1 %copy-start.1 = (f32[2048]{0:T(1024)S(1)}, f32[2048]{0:T(1024)}, u32[]{:S(2)}) copy-start(f32[2048]{0:T(1024)} %param.11) | copy-start | bytes 24580
  6.5 52.1 %copy-start.2 = (s32[1,6,2]{1,2,0:T(2,128)S(1)}, s32[1,6,2]{1,2,0:T(2,128)}, u32[]{:S(2)}) copy-start(s32[1,6,2]{1,2,0:T(2,128)} %param.12) | copy-start | bytes 148
  6.5 525.5 %all-reduce.2.cloned.1.call-start = ((), (), s32[]{:S(2)}) async-start(), calls=%async_computation | async-start | bytes 6291456 | tf_op jit(solution)/shard_map/psum | solution.py:84
  10.3 56.1 %collective-permute-start.2 = (f32[2,1,64,4096]{3,2,1,0:T(8,128)}, f32[2,1,64,4096]{3,2,1,0:T(8,128)S(1)}, u32[]{:S(2)}, u32[]{:S(2)}) collective-permute-start(f32[2,1,64,4096]{3,2,1,0:T(8,128)} %broadcast_multiply_fusion), channel_id=1, source_target_pairs={{0,1},{1,2},{2,3},{3,4},{4,5},{5,6},{6,7},{8,9},{9,10},{10,11},{11... | collective-permute-start | bytes 6291464 | tf_op jit(solution)/shard_map/ppermute | solution.py:16
  15.3 51.2 %collective-permute-start.3 = (f32[2,1,64,4096]{3,2,1,0:T(8,128)}, f32[2,1,64,4096]{3,2,1,0:T(8,128)}, u32[]{:S(2)}, u32[]{:S(2)}) collective-permute-start(f32[2,1,64,4096]{3,2,1,0:T(8,128)} %broadcast_multiply_fusion), channel_id=1, source_target_pairs={{1,0},{2,1},{3,2},{4,3},{5,4},{6,5},{7,6},{9,8},{10,9},{11,10},{12... | collective-permute-start | bytes 6291464 | tf_op jit(solution)/shard_map/ppermute | solution.py:19
  17.3 41.4 %collective-permute-start = (f32[1,1]{1,0:T(1,128)}, f32[1,1]{1,0:T(1,128)}, u32[]{:S(2)}, u32[]{:S(2)}) collective-permute-start(f32[1,1]{1,0:T(1,128)} %convert_element_type.35), channel_id=1, source_target_pairs={{0,1},{1,2},{2,3},{3,4},{4,5},{5,6},{6,7},{8,9},{9,10},{10,11},{11... | collective-permute-start | bytes 20 | tf_op jit(solution)/shard_map/ppermute | solution.py:16
  57.3 7.8 %collective-permute-start.1 = (f32[1,1]{1,0:T(1,128)}, f32[1,1]{1,0:T(1,128)}, u32[]{:S(2)}, u32[]{:S(2)}) collective-permute-start(f32[1,1]{1,0:T(1,128)} %convert_element_type.35), channel_id=1, source_target_pairs={{1,0},{2,1},{3,2},{4,3},{5,4},{6,5},{7,6},{9,8},{10,9},{11,10},{12... | collective-permute-start | bytes 20 | tf_op jit(solution)/shard_map/ppermute | solution.py:19
Sparse Core Ops, SparseCore 0:
  325.8 206.2 all-reduce.1
where the time goes:
time: 543 us; the launch traced here: 540 us
  matrix products  164 us (30%)
  blocking collectives  126 us (23%)
  waiting for transfers between devices  86.5 us (16%)
  starting transfers between devices  47.6 us (9%)
  loops' own time  44.1 us (8%)
  local copies, waits for them, and re-layouts  36.5 us (7%)
  other arithmetic  20.9 us (4%)
  between operations  14.2 us (3%)
    dot_general x8, matrix products, one_block(): lax.dot_general(lag_table, stack_rows, (((1,), (1,)), ((), ())), preferre...  164 us
    psum x1, blocking collectives, on_device(): totals = lax.psum(kept_counts, 'win')  126 us
    psum x1, waiting for transfers between devices, on_device(): whole_term = lax.psum(pieces.reshape(LAGS, stack_rows.shape[0]), 'win')  80.1 us
    ppermute x2, starting transfers between devices, padded(): lax.ppermute(lax.slice_in_dim(block, block.shape[dim] - width, None, axis...  45 us
    another operation x1, loops' own time, on_device(): lax.map(one_slot, (first_local, second_local, jnp.arange(slot_total, dtyp...  38.6 us
    squeeze x6, local copies, waits for them, and re-layouts, one_slot(): lax.dynamic_index_in_dim(extended, left_index, 1, keepdims=False)  15.3 us
    dynamic_slice x18, local copies, waits for them, and re-layouts, on_device(): lax.map(one_slot, (first_local, second_local, jnp.arange(slot_total, dtyp...  11.8 us
  transfers between devices with their start and end apart: 5, of which 2 were waited for; matrix products, arithmetic and copies ran while one was open for 0% of the time, Pallas kernels for 0%

commit v1 on v0

v1 whole, which is shorter than its diff:
```python
import math

import jax
import jax.numpy as jnp
import numpy as np
from jax import lax
from jax.experimental import pallas as pl
from jax.experimental.pallas import tpu as pltpu
from jax.sharding import PartitionSpec as P

LAGS = 2048
BINS = 2048
CHANNELS = 64
SLOTS = 6
ROWS = 8
PARTS = CHANNELS // ROWS
GROUP = 8
RING = 8
SHARE = LAGS // (GROUP * RING)
PIECE = SHARE * RING
HALF = PIECE // 2
KINDS = 3
LINES = KINDS * ROWS
AHEAD = 3
MESH = pl.DeviceIdType.MESH


def twiddles():
    frequency = np.arange(BINS, dtype=np.int64)[:, None]
    member = np.arange(2 * GROUP, dtype=np.int64)
    start = (member // 2) * SHARE + (member % 2) * (LAGS // 2) - LAGS // 2
    lane = np.arange(HALF, dtype=np.int64)
    place = (lane // SHARE) * PIECE + lane % SHARE

    def wave(offsets):
        angle = np.mod(frequency * offsets[None, :], 2 * BINS) * (math.pi / BINS)
        return np.cos(angle), np.sin(angle)

    start_cos, start_sin = wave(start)
    scale = math.sqrt(2.0 / BINS)
    place_cos, place_sin = wave(place)
    starts = np.zeros((BINS, 128), np.float32)
    starts[:, : 2 * GROUP] = start_cos
    starts[:, 2 * GROUP : 4 * GROUP] = start_sin
    places = np.concatenate([place_cos, place_sin], axis=1) * scale
    return starts, places.astype(np.float32)


def inverse_root(value):
    root = lax.rsqrt(value)
    return root * (1.5 - 0.5 * value * root * root)


def kernel(
    spectra, counts, band, pair_list, live, starts, places, out,
    own, low, high, first, second, table, stack, term, got_one, part, got_two, total,
    got_low, got_high, chosen, turned,
    count_own, count_low, count_high, kept, kept_one, kept_part, kept_two, kept_all, kept_low, kept_high,
    load_sem, halo_send, halo_recv, one_send, one_recv, two_send, two_recv, z_send, z_recv,
    count_send, count_recv, kept_one_send, kept_one_recv, kept_two_send, kept_two_recv, kept_z_send, kept_z_recv,
):
    win = lax.axis_index("win")
    plane = lax.axis_index("pair")
    row = win // GROUP
    member = win % GROUP
    above = (win, (plane + 1) % RING)
    below = (win, (plane + RING - 1) % RING)

    def in_group(step):
        return (row * GROUP + (member + step) % GROUP, plane)

    def in_ring(step):
        return (((row + step) % RING) * GROUP + member, plane)

    loads = [
        pltpu.make_async_copy(spectra.at[:, 0], own, load_sem.at[0]),
        pltpu.make_async_copy(starts, first, load_sem.at[1]),
        pltpu.make_async_copy(places, second, load_sem.at[2]),
    ]
    for load in loads:
        load.start()

    barrier = pltpu.get_barrier_semaphore()
    for neighbour in (above, below):
        pl.semaphore_signal(barrier, inc=1, device_id=neighbour, device_id_type=MESH)
    for step in range(1, GROUP):
        pl.semaphore_signal(barrier, inc=1, device_id=in_group(step), device_id_type=MESH)
    for step in range(1, RING):
        pl.semaphore_signal(barrier, inc=1, device_id=in_ring(step), device_id_type=MESH)
    count_own[...] = jnp.full((8, 128), counts[0, 0].astype(jnp.float32))
    pl.semaphore_wait(barrier, 2 + GROUP - 1 + RING - 1)

    def remote(source, target, send, recv, device):
        return pltpu.make_async_remote_copy(
            src_ref=source, dst_ref=target, send_sem=send, recv_sem=recv, device_id=device, device_id_type=MESH
        )

    def halo(index):
        block = spectra.at[:, 0, pl.ds(pl.multiple_of(index * ROWS, ROWS), ROWS), :]
        return (
            remote(block, low.at[index], halo_send.at[0, index], halo_recv.at[0, index], above),
            remote(block, high.at[index], halo_send.at[1, index], halo_recv.at[1, index], below),
        )

    count_copies = (
        remote(count_own, count_low, count_send.at[0], count_recv.at[0], above),
        remote(count_own, count_high, count_send.at[1], count_recv.at[1], below),
    )
    for copy in count_copies:
        copy.start()
    for index in range(AHEAD):
        for copy in halo(index):
            copy.start()

    loads[1].wait()
    loads[2].wait()
    stack[pl.ds(2 * 16 - 16, 16), :] = jnp.zeros((16, 2 * BINS), jnp.bfloat16)

    @pl.loop(0, BINS // 16)
    def _(block):
        rows = pl.ds(pl.multiple_of(block * 16, 16), 16)
        shifted = pl.ds(pl.multiple_of(block * 16 + BINS, 16), 16)
        place_cos = second[rows, 0:HALF]
        place_sin = second[rows, HALF : 2 * HALF]
        start_all = first[rows, :]
        for index in range(2 * GROUP):
            start_cos = start_all[:, index : index + 1]
            start_sin = start_all[:, 2 * GROUP + index : 2 * GROUP + index + 1]
            lanes = slice((index % 2) * HALF, (index % 2 + 1) * HALF)
            table[index // 2, rows, lanes] = (start_cos * place_cos - start_sin * place_sin).astype(jnp.bfloat16)
            table[index // 2, shifted, lanes] = (-(start_sin * place_cos) - start_cos * place_sin).astype(
                jnp.bfloat16
            )

    for copy in count_copies:
        copy.wait()
    mine = count_own[...]
    above_count = count_high[...]
    side = jnp.minimum(mine, above_count)
    across = jnp.minimum(count_low[...], above_count)
    line = lax.broadcasted_iota(jnp.int32, (8, 128), 0)
    kept[...] = jnp.where(line == 0, mine, jnp.where(line == 1, side, across))
    for step in range(1, GROUP):
        remote(kept, kept_one.at[step - 1], kept_one_send, kept_one_recv, in_group(step)).start()

    loads[0].wait()
    mask_own = jnp.where(mine > 1.5, 1.0, 0.0)
    mask_side = jnp.where(side > 1.5, 1.0, 0.0)
    mask_across = jnp.where(across > 1.5, 1.0, 0.0)

    def whole(ref, send, recv):
        return remote(ref, ref, send, recv, above)

    def correlate(index):
        for copy in halo(index):
            copy.wait_recv()

        @pl.when(index + AHEAD < PARTS)
        def _():
            for copy in halo(index + AHEAD):
                copy.start()

        here = pl.ds(pl.multiple_of(index * ROWS, ROWS), ROWS)

        def level(read):
            square = jnp.zeros((ROWS, 128), jnp.float32)
            for lane in range(0, 2 * BINS, 128):
                entry = read(slice(lane, lane + 128))
                square = square + entry * entry
            mean = jnp.sum(square, axis=1, keepdims=True) * (1.0 / (2 * BINS))
            return jnp.broadcast_to(inverse_root(mean + 1e-6), (ROWS, 128))

        def reader(kind, window):
            if kind == 0:
                return lambda lanes: own[window, here, lanes]
            ref = low if kind == 1 else high
            return lambda lanes: ref[index, window, :, lanes]

        readers = {(kind, window): reader(kind, window) for kind in range(3) for window in range(2)}
        levels = {key: level(read) for key, read in readers.items()}
        for lane in range(0, BINS, 128):
            real, imag = slice(lane, lane + 128), slice(BINS + lane, BINS + lane + 128)
            weight = jnp.broadcast_to(band[:, real], (ROWS, 128))
            re = {key: read(real) * levels[key] for key, read in readers.items()}
            im = {key: read(imag) * levels[key] for key, read in readers.items()}

            def cross(a, b, mask):
                parts = []
                for window in range(2):
                    ra, ia, rb, ib = re[a, window], im[a, window], re[b, window], im[b, window]
                    parts.append((ra * rb + ia * ib, ia * rb - ra * ib))
                return (
                    (parts[0][0] + mask * parts[1][0]) * weight,
                    (parts[0][1] + mask * parts[1][1]) * weight,
                )

            power = (re[0, 0] * re[0, 0] + im[0, 0] * im[0, 0]) + mask_own * (
                re[0, 1] * re[0, 1] + im[0, 1] * im[0, 1]
            )
            side_re, side_im = cross(0, 2, mask_side)
            across_re, across_im = cross(1, 2, mask_across)
            zero = jnp.zeros_like(power)
            stack[0:16, real] = jnp.concatenate([power * weight, side_re], axis=0).astype(jnp.bfloat16)
            stack[0:16, imag] = jnp.concatenate([zero, side_im], axis=0).astype(jnp.bfloat16)
            stack[16:32, real] = jnp.concatenate([across_re, zero], axis=0).astype(jnp.bfloat16)
            stack[16:32, imag] = jnp.concatenate([across_im, zero], axis=0).astype(jnp.bfloat16)

        def piece(step):
            product = lax.dot_general(
                stack[...],
                table[(member + step) % GROUP],
                (((1,), (0,)), ((), ())),
                preferred_element_type=jnp.float32,
            )
            term[index, step] = product[:LINES]

        @pl.loop(1, GROUP)
        def _(step):
            piece(step)
            remote(
                term.at[index, step], got_one.at[index, step - 1], one_send.at[index], one_recv.at[index], in_group(step)
            ).start()

        piece(0)

    def add_group(index):
        whole(got_one.at[index], one_send.at[index], one_recv.at[index]).wait_recv()
        for half in range(2):
            lanes = slice(half * HALF, (half + 1) * HALF)
            value = term[index, 0, :, lanes]
            for step in range(GROUP - 1):
                value = value + got_one[index, step, :, lanes]
            part[index, half] = value
        for step in range(1, RING):
            target = (row + step) % RING
            remote(
                part.at[index, target // (RING // 2)], got_two.at[index, step - 1],
                two_send.at[index], two_recv.at[index], in_ring(step),
            ).start()

    def z_copies(index):
        return (
            remote(total.at[index, pl.ds(0, 16)], got_low.at[index], z_send.at[0, index], z_recv.at[0, index], above),
            remote(total.at[index, pl.ds(0, 8)], got_high.at[index], z_send.at[1, index], z_recv.at[1, index], below),
        )

    def add_ring(index):
        whole(got_two.at[index], two_send.at[index], two_recv.at[index]).wait_recv()
        value = part[index, row // (RING // 2)]
        for step in range(RING - 1):
            value = value + got_two[index, step]
        total[index] = value
        for copy in z_copies(index):
            copy.start()

    def choose(options, slot):
        a, b = pair_list[0, slot, 0], pair_list[0, slot, 1]
        value = options[0]
        value = jnp.where((a == plane - 1) & (b == plane), options[1], value)
        value = jnp.where((a == plane - 1) & (b == plane + 1), options[2], value)
        value = jnp.where((a == plane) & (b == plane), options[3], value)
        value = jnp.where((a == plane) & (b == plane + 1), options[4], value)
        return jnp.where((a == plane + 1) & (b == plane + 1), options[5], value)

    def place_slots(index):
        for copy in z_copies(index):
            copy.wait()
        whole(term.at[index, pl.ds(1, GROUP - 1)], one_send.at[index], one_recv.at[index]).wait_send()
        whole(got_two.at[index], two_send.at[index], two_recv.at[index]).wait_send()
        for copy in halo(index):
            copy.wait_send()
        options = [
            got_low[index, 0:8], got_low[index, 8:16], total[index, 16:24],
            total[index, 0:8], total[index, 8:16], got_high[index],
        ]
        for slot in range(SLOTS):
            chosen[pl.ds(pl.multiple_of(slot * CHANNELS + index * ROWS, ROWS), ROWS), :] = choose(options, slot)

    def kept_copies():
        return (
            remote(kept_all, kept_low, kept_z_send.at[0], kept_z_recv.at[0], above),
            remote(kept_all, kept_high, kept_z_send.at[1], kept_z_recv.at[1], below),
        )

    @pl.loop(0, PARTS + 3)
    def _(turn):
        @pl.when(turn < PARTS)
        def _():
            correlate(turn)

        @pl.when((turn >= 1) & (turn < PARTS + 1))
        def _():
            add_group(turn - 1)

        @pl.when(turn == 1)
        def _():
            whole(kept_one, kept_one_send, kept_one_recv).wait()
            value = kept[...]
            for step in range(GROUP - 1):
                value = value + kept_one[step]
            kept_part[...] = value
            for step in range(1, RING):
                remote(kept_part, kept_two.at[step - 1], kept_two_send, kept_two_recv, in_ring(step)).start()

        @pl.when((turn >= 2) & (turn < PARTS + 2))
        def _():
            add_ring(turn - 2)

        @pl.when(turn == 3)
        def _():
            whole(kept_two, kept_two_send, kept_two_recv).wait()
            value = kept_part[...]
            for step in range(RING - 1):
                value = value + kept_two[step]
            kept_all[...] = value
            for copy in kept_copies():
                copy.start()

        @pl.when(turn == 5)
        def _():
            for copy in kept_copies():
                copy.wait()

        @pl.when(turn >= 3)
        def _():
            place_slots(turn - 3)

    kept_options = [
        kept_low[0:1], kept_low[1:2], kept_all[2:3], kept_all[0:1], kept_all[1:2], kept_high[0:1],
    ]
    for slot in range(SLOTS):
        alive = (slot < live[0]).astype(jnp.float32)
        scale = alive / choose(kept_options, slot)
        rows = slice(slot * CHANNELS, (slot + 1) * CHANNELS)
        chosen[rows, :] = chosen[rows, :] * scale
    for block in range(SLOTS * CHANNELS // 128):
        turned[:, block * 128 : (block + 1) * 128] = chosen[block * 128 : (block + 1) * 128, :].T
    out[...] = turned[pl.ds(pl.multiple_of((row % (RING // 2)) * SHARE, SHARE), SHARE), :]


def on_device(spectra, counts, band_filter, pair_list, live_slots):
    starts, places = twiddles()
    f32 = jnp.float32
    dma = pltpu.SemaphoreType.DMA
    tile = (8, 128)
    return pl.pallas_call(
        kernel,
        out_shape=jax.ShapeDtypeStruct((SHARE, SLOTS * CHANNELS), f32),
        in_specs=[
            pl.BlockSpec(memory_space=pl.ANY),
            pl.BlockSpec(memory_space=pltpu.SMEM),
            pl.BlockSpec(memory_space=pltpu.VMEM),
            pl.BlockSpec(memory_space=pltpu.SMEM),
            pl.BlockSpec(memory_space=pltpu.SMEM),
            pl.BlockSpec(memory_space=pl.ANY),
            pl.BlockSpec(memory_space=pl.ANY),
        ],
        out_specs=pl.BlockSpec(memory_space=pltpu.VMEM),
        scratch_shapes=[
            pltpu.VMEM((2, CHANNELS, 2 * BINS), f32),
            pltpu.VMEM((PARTS, 2, ROWS, 2 * BINS), f32),
            pltpu.VMEM((PARTS, 2, ROWS, 2 * BINS), f32),
            pltpu.VMEM((BINS, 128), f32),
            pltpu.VMEM((BINS, 2 * HALF), f32),
            pltpu.VMEM((GROUP, 2 * BINS, PIECE), jnp.bfloat16),
            pltpu.VMEM((32, 2 * BINS), jnp.bfloat16),
            pltpu.VMEM((PARTS, GROUP, LINES, PIECE), f32),
            pltpu.VMEM((PARTS, GROUP - 1, LINES, PIECE), f32),
            pltpu.VMEM((PARTS, 2, LINES, HALF), f32),
            pltpu.VMEM((PARTS, RING - 1, LINES, HALF), f32),
            pltpu.VMEM((PARTS, LINES, HALF), f32),
            pltpu.VMEM((PARTS, 2 * ROWS, HALF), f32),
            pltpu.VMEM((PARTS, ROWS, HALF), f32),
            pltpu.VMEM((SLOTS * CHANNELS, HALF), f32),
            pltpu.VMEM((HALF, SLOTS * CHANNELS), f32),
            pltpu.VMEM(tile, f32),
            pltpu.VMEM(tile, f32),
            pltpu.VMEM(tile, f32),
            pltpu.VMEM(tile, f32),
            pltpu.VMEM((GROUP - 1,) + tile, f32),
            pltpu.VMEM(tile, f32),
            pltpu.VMEM((RING - 1,) + tile, f32),
            pltpu.VMEM(tile, f32),
            pltpu.VMEM(tile, f32),
            pltpu.VMEM(tile, f32),
            dma((3,)),
            dma((2, PARTS)), dma((2, PARTS)),
            dma((PARTS,)), dma((PARTS,)),
            dma((PARTS,)), dma((PARTS,)),
            dma((2, PARTS)), dma((2, PARTS)),
            dma((2,)), dma((2,)),
            dma, dma, dma, dma,
            dma((2,)), dma((2,)),
        ],
        compiler_params=pltpu.CompilerParams(
            collective_id=0, has_side_effects=True, vmem_limit_bytes=56 * 1024 * 1024
        ),
    )(spectra, counts, band_filter.reshape(1, BINS), pair_list, live_slots, jnp.asarray(starts), jnp.asarray(places))


def solution(mesh):
    placed = (P("win", "pair", None, None), P("win", "pair"), P(), P("pair", None, None), P("pair"))
    return jax.shard_map(
        on_device, mesh=mesh, in_specs=placed, out_specs=P("win", "pair"), check_vma=False
    )
```

time: 543 us -> 95.2 us (0.18)
  matrix products: 164 us -> 0 us
  blocking collectives: 126 us -> 0 us
  Pallas kernels: 0 us -> 90.9 us
  waiting for transfers between devices: 86.5 us -> 0 us
  starting transfers between devices: 47.6 us -> 0 us
  loops' own time: 44.1 us -> 0 us
  local copies, waits for them, and re-layouts: 36.5 us -> 2.77 us
  other arithmetic: 20.9 us -> 0 us
  between operations: 14.2 us -> 1.31 us
    dot_general x8 -> x0, matrix products: 164 us -> none  [one_block(): lax.dot_general(lag_table, stack_rows, (((1,), (1,)), ((), ())), preferre...]
    psum x1 -> x0, blocking collectives: 126 us -> none  [on_device(): totals = lax.psum(kept_counts, 'win')]
    pallas_call x0 -> x1, Pallas kernels: none -> 90.9 us  [on_device(): pl.pallas_call(kernel, out_shape=jax.ShapeDtypeStruct((SHARE, SLOTS * CHA...]
    psum x1 -> x0, waiting for transfers between devices: 80.1 us -> none  [on_device(): whole_term = lax.psum(pieces.reshape(LAGS, stack_rows.shape[0]), 'win')]
    ppermute x4 -> x0, starting transfers between devices: 47.6 us -> none  [the longest x2 45 us: padded(): lax.ppermute(lax.slice_in_dim(block, block.shape[dim] - width, None, axis...]
    another operation x2 -> x0, loops' own time: 44.1 us -> none  [the longest x1 38.6 us: on_device(): lax.map(one_slot, (first_local, second_local, jnp.arange(slot_total, dtyp...]
    dynamic_slice x32 -> x0, local copies, waits for them, and re-layouts: 20.7 us -> none  [the longest x18 11.8 us: on_device(): lax.map(one_slot, (first_local, second_local, jnp.arange(slot_total, dtyp...]
    squeeze x6 -> x0, local copies, waits for them, and re-layouts: 15.3 us -> none  [one_slot(): lax.dynamic_index_in_dim(extended, left_index, 1, keepdims=False)]
  transfers between devices with their start and end apart: 5 -> 0, of which waited for: 2 -> 0; matrix products, arithmetic and copies ran while one was open for 0% -> 0% of each run, Pallas kernels for 0% -> 0%
where the time goes in v1:
time: 95.2 us; the launch traced here: 95 us
  Pallas kernels  90.9 us (95%)
  local copies, waits for them, and re-layouts  2.77 us (3%)
  between operations  1.31 us (1%)
    pallas_call x1, Pallas kernels, on_device(): pl.pallas_call(kernel, out_shape=jax.ShapeDtypeStruct((SHARE, SLOTS * CHA...  90.9 us
    unnamed x2, local copies, waits for them, and re-layouts  2.77 us

profile of v1, /device:TPU:1, one launch (start us, length us, event | category | flops | bytes accessed | tf_op | source)
XLA Modules:
  0.0 95.0 jit_solution(9269332233682298839)
XLA Ops:
  1.3 1.4 %copy.8.pair_list = s32[1,6,2]{2,1,0:T(8,128)} copy(s32[1,6,2]{1,2,0:T(2,128)} %param.10) | data formatting | bytes 96 | tf_op args[3]
  2.6 90.9 %shard_map.73 = f32[32,384]{1,0:T(8,128)} custom-call(f32[2,1,64,4096]{3,2,1,0:T(8,128)} %spectra.1, s32[1,1]{1,0:T(1,128)S(6)} %copy.10.counts, f32[1,2048]{1,0:T(1,128)} %bitcast.1, s32[1,6,2]{2,1,0:T(8,128)} %copy.8.pair_list, s32[1]{0:T(128)S(6)} %copy.11.live, f32[2048,128]{1,0:T(8,128)} %constant.4.clone.starts, f32[2048,256]{1,0:T(8,128)} %constant.5.clone.places), custom_call_target="tpu_custom_call" | custom-call | tf_op jit(solution)/shard_map/pallas_call | solution.py:346
  93.5 1.4 %copy.12 = f32[32,384]{1,0:T(8,128)} copy(f32[32,384]{1,0:T(8,128)} %shard_map.73) | data formatting | bytes 98304

commit v2 on v1

v2 whole, which is shorter than its diff:
```python
import math

import jax
import jax.numpy as jnp
import numpy as np
from jax import lax
from jax.experimental import pallas as pl
from jax.experimental.pallas import tpu as pltpu
from jax.sharding import PartitionSpec as P

LAGS = 2048
BINS = 2048
CHANNELS = 64
SLOTS = 6
ROWS = 8
PARTS = CHANNELS // ROWS
GROUP = 8
RING = 8
SHARE = LAGS // (GROUP * RING)
PIECE = SHARE * RING
HALF = PIECE // 2
LINES = 2 * ROWS
AHEAD = 3
MESH = pl.DeviceIdType.MESH


def twiddles():
    frequency = np.arange(BINS, dtype=np.int64)[:, None]
    lane = np.arange(HALF, dtype=np.int64)
    place = (lane // SHARE) * PIECE + lane % SHARE

    def wave(offsets):
        angle = np.mod(frequency * offsets[None, :], 2 * BINS) * (math.pi / BINS)
        return np.cos(angle), np.sin(angle)

    turns = np.zeros((BINS, 128), np.float32)
    turn_cos, turn_sin = wave(np.array([SHARE], np.int64))
    turns[:, 0:1], turns[:, 1:2] = turn_cos, turn_sin
    place_cos, place_sin = wave(place)
    places = np.concatenate([place_cos, -place_sin], axis=1) * math.sqrt(2.0 / BINS)
    return turns, places.astype(np.float32)


def inverse_root(value):
    root = lax.rsqrt(value)
    return root * (1.5 - 0.5 * value * root * root)


def kernel(
    spectra, counts_hbm, band, pairs_hbm, live_hbm, turns, places, out,
    counts, pairs, live,
    own, own_level, low, high, turn_table, place_table, table,
    own_stack, own_term, own_got_one, own_pack, own_got_two, own_total, own_low, own_high, own_wide,
    stack, term, got_one, pack, got_two, total, got_low, chosen,
    count_own, count_low, count_high, kept, kept_one, kept_part, kept_two, kept_all, kept_low, kept_high,
    load_sem, halo_send, halo_recv, one_send, one_recv, two_send, two_recv, z_send, z_recv,
    own_one_send, own_one_recv, own_two_send, own_two_recv, own_z_send, own_z_recv,
    count_send, count_recv, kept_one_send, kept_one_recv, kept_two_send, kept_two_recv, kept_z_send, kept_z_recv,
):
    win = lax.axis_index("win")
    plane = lax.axis_index("pair")
    row = win // GROUP
    member = win % GROUP
    above = (win, (plane + 1) % RING)
    below = (win, (plane + RING - 1) % RING)

    def in_group(step):
        return (row * GROUP + (member + step) % GROUP, plane)

    def in_ring(step):
        return (((row + step) % RING) * GROUP + member, plane)

    barrier = pltpu.get_barrier_semaphore()
    for neighbour in (above, below):
        pl.semaphore_signal(barrier, inc=1, device_id=neighbour, device_id_type=MESH)
    for step in range(1, GROUP):
        pl.semaphore_signal(barrier, inc=1, device_id=in_group(step), device_id_type=MESH)
    for step in range(1, RING):
        pl.semaphore_signal(barrier, inc=1, device_id=in_ring(step), device_id_type=MESH)

    count_load = pltpu.make_async_copy(counts_hbm, counts, load_sem.at[0])
    pairs_load = pltpu.make_async_copy(pairs_hbm, pairs, load_sem.at[1])
    live_load = pltpu.make_async_copy(live_hbm, live, load_sem.at[2])
    turn_load = pltpu.make_async_copy(turns, turn_table, load_sem.at[3])
    place_load = pltpu.make_async_copy(places, place_table, load_sem.at[4])
    own_load = pltpu.make_async_copy(spectra.at[:, 0], own, load_sem.at[5])
    for load in (count_load, pairs_load, live_load, turn_load, place_load, own_load):
        load.start()
    count_load.wait()
    count_own[...] = jnp.full((8, 128), counts[0, 0].astype(jnp.float32))
    pl.semaphore_wait(barrier, 2 + GROUP - 1 + RING - 1)

    def remote(source, target, send, recv, device):
        return pltpu.make_async_remote_copy(
            src_ref=source, dst_ref=target, send_sem=send, recv_sem=recv, device_id=device, device_id_type=MESH
        )

    def whole(ref, send, recv):
        return remote(ref, ref, send, recv, above)

    def halo(index):
        block = spectra.at[:, 0, pl.ds(pl.multiple_of(index * ROWS, ROWS), ROWS), :]
        return (
            remote(block, low.at[index], halo_send.at[0, index], halo_recv.at[0, index], above),
            remote(block, high.at[index], halo_send.at[1, index], halo_recv.at[1, index], below),
        )

    def both_sides(source, to_above, to_below, send, recv):
        return (
            remote(source, to_above, send.at[0], recv.at[0], above),
            remote(source, to_below, send.at[1], recv.at[1], below),
        )

    count_copies = both_sides(count_own, count_low, count_high, count_send, count_recv)
    for copy in count_copies:
        copy.start()
    for index in range(AHEAD):
        for copy in halo(index):
            copy.start()

    turn_load.wait()
    place_load.wait()
    line = lax.broadcasted_iota(jnp.int32, (16, 128), 0)
    odd = (line % 2) == 1
    sign_sin = jnp.where(line % 4 < 2, 1.0, -1.0)
    sign_cos = jnp.where((line % 4 == 0) | (line % 4 == 3), 1.0, -1.0)

    @pl.loop(0, BINS // 16, unroll=2)
    def _(block):
        rows = pl.ds(pl.multiple_of(block * 16, 16), 16)
        shifted = pl.ds(pl.multiple_of(block * 16 + BINS, 16), 16)
        cos = place_table[rows, 0:HALF]
        minus_sin = place_table[rows, HALF : 2 * HALF]
        turn_cos = jnp.broadcast_to(turn_table[rows, 0:1], (16, 128))
        turn_sin = jnp.broadcast_to(turn_table[rows, 1:2], (16, 128))
        for index in range(GROUP):
            table[index, rows, HALF : 2 * HALF] = cos.astype(jnp.bfloat16)
            table[index, shifted, HALF : 2 * HALF] = minus_sin.astype(jnp.bfloat16)
            table[index, rows, 0:HALF] = (jnp.where(odd, minus_sin, cos) * sign_cos).astype(jnp.bfloat16)
            table[index, shifted, 0:HALF] = (jnp.where(odd, cos, minus_sin) * sign_sin).astype(jnp.bfloat16)
            if index < GROUP - 1:
                cos, minus_sin = (
                    cos * turn_cos + minus_sin * turn_sin,
                    minus_sin * turn_cos - cos * turn_sin,
                )

    def level(read, rows):
        square = jnp.zeros((rows, 128), jnp.float32)
        for lane in range(0, 2 * BINS, 128):
            entry = read(slice(lane, lane + 128))
            square = square + entry * entry
        mean = jnp.sum(square, axis=1, keepdims=True) * (1.0 / (2 * BINS))
        return jnp.broadcast_to(inverse_root(mean + 1e-6), (rows, 128))

    own_load.wait()
    mine = count_own[...]
    mask_own = jnp.concatenate([jnp.where(mine > 1.5, 1.0, 0.0)] * 2, axis=0)

    @pl.loop(0, CHANNELS // 16)
    def _(block):
        here = pl.ds(pl.multiple_of(block * 16, 16), 16)
        levels = []
        for window in range(2):
            levels.append(level(lambda lanes: own[window, here, lanes], 16))
            own_level[window, here, :] = levels[window]
        for lane in range(0, BINS, 128):
            real, imag = slice(lane, lane + 128), slice(BINS + lane, BINS + lane + 128)
            powers = []
            for window in range(2):
                re, im = own[window, here, real] * levels[window], own[window, here, imag] * levels[window]
                powers.append(re * re + im * im)
            weight = jnp.broadcast_to(band[:, real], (16, 128))
            own_stack[here, real] = ((powers[0] + mask_own * powers[1]) * weight).astype(jnp.bfloat16)

    def own_piece(step):
        own_term[step] = lax.dot_general(
            own_stack[...],
            table[(member + step) % GROUP, 0:BINS],
            (((1,), (0,)), ((), ())),
            preferred_element_type=jnp.float32,
        )

    @pl.loop(1, GROUP)
    def _(step):
        own_piece(step)
        remote(own_term.at[step], own_got_one.at[step - 1], own_one_send, own_one_recv, in_group(step)).start()

    own_piece(0)

    for copy in count_copies:
        copy.wait()
    above_count = count_high[...]
    side = jnp.minimum(mine, above_count)
    across = jnp.minimum(count_low[...], above_count)
    row_line = lax.broadcasted_iota(jnp.int32, (8, 128), 0)
    kept[...] = jnp.where(row_line == 0, mine, jnp.where(row_line == 1, side, across))
    for step in range(1, GROUP):
        remote(kept, kept_one.at[step - 1], kept_one_send, kept_one_recv, in_group(step)).start()
    mask_side = jnp.where(side > 1.5, 1.0, 0.0)
    mask_across = jnp.where(across > 1.5, 1.0, 0.0)

    def correlate(index):
        for copy in halo(index):
            copy.wait_recv()

        @pl.when(index + AHEAD < PARTS)
        def _():
            for copy in halo(index + AHEAD):
                copy.start()

        here = pl.ds(pl.multiple_of(index * ROWS, ROWS), ROWS)

        def reader(kind, window):
            if kind == 0:
                return lambda lanes: own[window, here, lanes]
            ref = low if kind == 1 else high
            return lambda lanes: ref[index, window, :, lanes]

        readers = {(kind, window): reader(kind, window) for kind in range(3) for window in range(2)}
        levels = {
            key: own_level[key[1], here, :] if key[0] == 0 else level(read, ROWS) for key, read in readers.items()
        }
        for lane in range(0, BINS, 128):
            real, imag = slice(lane, lane + 128), slice(BINS + lane, BINS + lane + 128)
            weight = jnp.broadcast_to(band[:, real], (ROWS, 128))
            re = {key: read(real) * levels[key] for key, read in readers.items()}
            im = {key: read(imag) * levels[key] for key, read in readers.items()}

            def cross(a, b, mask):
                parts = []
                for window in range(2):
                    ra, ia, rb, ib = re[a, window], im[a, window], re[b, window], im[b, window]
                    parts.append((ra * rb + ia * ib, ia * rb - ra * ib))
                return (
                    (parts[0][0] + mask * parts[1][0]) * weight,
                    (parts[0][1] + mask * parts[1][1]) * weight,
                )

            side_re, side_im = cross(0, 2, mask_side)
            across_re, across_im = cross(1, 2, mask_across)
            stack[:, real] = jnp.concatenate([side_re, across_re], axis=0).astype(jnp.bfloat16)
            stack[:, imag] = jnp.concatenate([side_im, across_im], axis=0).astype(jnp.bfloat16)

        def piece(step):
            term[index, step] = lax.dot_general(
                stack[...],
                table[(member + step) % GROUP],
                (((1,), (0,)), ((), ())),
                preferred_element_type=jnp.float32,
            )

        @pl.loop(1, GROUP)
        def _(step):
            piece(step)
            remote(
                term.at[index, step], got_one.at[index, step - 1], one_send.at[index], one_recv.at[index], in_group(step)
            ).start()

        piece(0)

    def packed(groups, chip):
        lane = lax.broadcasted_iota(jnp.int32, groups[0].shape, 1)
        value = None
        for place in reversed(range(len(groups))):
            shift = ((place - chip) * SHARE) % 128
            moved = pltpu.roll(groups[place], shift, axis=1) if shift else groups[place]
            value = moved if value is None else jnp.where(lane < (place + 1) * SHARE, moved, value)
        return value

    def add_group(index):
        whole(got_one.at[index], one_send.at[index], one_recv.at[index]).wait_recv()
        for half in range(2):
            lanes = slice(half * HALF, (half + 1) * HALF)
            value = term[index, 0, :, lanes]
            for step in range(GROUP - 1):
                value = value + got_one[index, step, :, lanes]
            for chip in range(RING // 2):
                pack[index, half * (RING // 2) + chip] = packed([value[:ROWS], value[ROWS:]], chip)
        for step in range(1, RING):
            remote(
                pack.at[index, (row + step) % RING], got_two.at[index, step - 1],
                two_send, two_recv.at[index], in_ring(step),
            ).start()

    def add_ring(index):
        whole(got_two.at[index], two_send, two_recv.at[index]).wait_recv()
        value = pack[index, row]
        for step in range(RING - 1):
            value = value + got_two[index, step]
        total[index] = value
        remote(total.at[index], got_low.at[index], z_send, z_recv, above).start()
        whole(got_one.at[index], one_send.at[index], one_recv.at[index]).wait_send()
        for copy in halo(index):
            copy.wait_send()

    @pl.loop(0, PARTS + 2)
    def _(turn):
        @pl.when(turn < PARTS)
        def _():
            correlate(turn)

        @pl.when((turn >= 1) & (turn < PARTS + 1))
        def _():
            add_group(turn - 1)

        @pl.when(turn >= 2)
        def _():
            add_ring(turn - 2)

        @pl.when(turn == 2)
        def _():
            whole(kept_one, kept_one_send, kept_one_recv).wait()
            value = kept[...]
            for step in range(GROUP - 1):
                value = value + kept_one[step]
            kept_part[...] = value
            whole(own_got_one, own_one_send, own_one_recv).wait()
            for half in range(2):
                lanes = slice(half * HALF, (half + 1) * HALF)
                groups = []
                for block in range(4):
                    rows = slice(block * 16, (block + 1) * 16)
                    value = own_term[0, rows, lanes]
                    for step in range(GROUP - 1):
                        value = value + own_got_one[step, rows, lanes]
                    groups.append(value)
                for chip in range(RING // 2):
                    own_pack[half * (RING // 2) + chip] = packed(groups, chip)
            for step in range(1, RING):
                remote(kept_part, kept_two.at[step - 1], kept_two_send, kept_two_recv, in_ring(step)).start()
                remote(
                    own_pack.at[(row + step) % RING], own_got_two.at[step - 1], own_two_send, own_two_recv, in_ring(step)
                ).start()

        @pl.when(turn == 4)
        def _():
            whole(kept_two, kept_two_send, kept_two_recv).wait()
            whole(own_got_two, own_two_send, own_two_recv).wait()
            value = kept_part[...]
            own_value = own_pack[row]
            for step in range(RING - 1):
                value = value + kept_two[step]
                own_value = own_value + own_got_two[step]
            kept_all[...] = value
            own_total[...] = own_value
            for copy in both_sides(kept_all, kept_low, kept_high, kept_z_send, kept_z_recv):
                copy.start()
            for copy in both_sides(own_total, own_low, own_high, own_z_send, own_z_recv):
                copy.start()

        @pl.when(turn == 6)
        def _():
            for copy in both_sides(kept_all, kept_low, kept_high, kept_z_send, kept_z_recv):
                copy.wait()
            for copy in both_sides(own_total, own_low, own_high, own_z_send, own_z_recv):
                copy.wait()
            for place, source in enumerate((own_low, own_total, own_high)):
                value = source[...]
                for block in range(4):
                    rows = slice(block * 16, (block + 1) * 16)
                    own_wide[place, rows, :] = pltpu.roll(value, 128 - block * SHARE, axis=1) if block else value

    pairs_load.wait()
    live_load.wait()
    whole(got_two, two_send, two_recv.at[0]).wait_send()
    whole(got_low, z_send, z_recv).wait()
    kept_options = [
        kept_low[0:1], kept_low[1:2], kept_all[2:3], kept_all[0:1], kept_all[1:2], kept_high[0:1],
    ]
    for slot in range(SLOTS):
        a, b = pairs[0, 0, slot], pairs[0, 1, slot]
        tests = [
            (a == plane - 1) & (b == plane),
            (a == plane - 1) & (b == plane + 1),
            (a == plane) & (b == plane),
            (a == plane) & (b == plane + 1),
            (a == plane + 1) & (b == plane + 1),
        ]

        def choose(options):
            value = options[0]
            for test, option in zip(tests, options[1:]):
                value = jnp.where(test, option, value)
            return value

        alive = (slot < live[0]).astype(jnp.float32)
        scale = jnp.broadcast_to(alive / choose(kept_options), (ROWS, 128))
        for index in range(PARTS):
            rows = slice(index * ROWS, (index + 1) * ROWS)
            value = choose([
                own_wide[0, rows], got_low[index], pltpu.roll(total[index], 128 - SHARE, axis=1),
                own_wide[1, rows], total[index], own_wide[2, rows],
            ])
            chosen[slot * CHANNELS + index * ROWS : slot * CHANNELS + (index + 1) * ROWS, :] = value * scale
    for block in range(SLOTS * CHANNELS // 128):
        lanes = slice(block * 128, (block + 1) * 128)
        out[:, lanes] = chosen[lanes, :].T[:SHARE]


def on_device(spectra, counts, band_filter, pair_list, live_slots):
    turns, places = twiddles()
    f32, bf16, i32 = jnp.float32, jnp.bfloat16, jnp.int32
    dma = pltpu.SemaphoreType.DMA
    tile = (8, 128)
    vmem = pltpu.VMEM
    anywhere = pl.BlockSpec(memory_space=pl.ANY)
    return pl.pallas_call(
        kernel,
        out_shape=jax.ShapeDtypeStruct((SHARE, SLOTS * CHANNELS), f32),
        in_specs=[anywhere, anywhere, pl.BlockSpec(memory_space=vmem), anywhere, anywhere, anywhere, anywhere],
        out_specs=pl.BlockSpec(memory_space=vmem),
        scratch_shapes=[
            pltpu.SMEM((1, 1), i32), pltpu.SMEM((1, 2, SLOTS), i32), pltpu.SMEM((1,), i32),
            vmem((2, CHANNELS, 2 * BINS), f32),
            vmem((2, CHANNELS, 128), f32),
            vmem((PARTS, 2, ROWS, 2 * BINS), f32),
            vmem((PARTS, 2, ROWS, 2 * BINS), f32),
            vmem((BINS, 128), f32),
            vmem((BINS, 2 * HALF), f32),
            vmem((GROUP, 2 * BINS, PIECE), bf16),
            vmem((CHANNELS, BINS), bf16),
            vmem((GROUP, CHANNELS, PIECE), f32),
            vmem((GROUP - 1, CHANNELS, PIECE), f32),
            vmem((RING, 16, 128), f32),
            vmem((RING - 1, 16, 128), f32),
            vmem((16, 128), f32), vmem((16, 128), f32), vmem((16, 128), f32),
            vmem((3, CHANNELS, 128), f32),
            vmem((LINES, 2 * BINS), bf16),
            vmem((PARTS, GROUP, LINES, PIECE), f32),
            vmem((PARTS, GROUP - 1, LINES, PIECE), f32),
            vmem((PARTS, RING) + tile, f32),
            vmem((PARTS, RING - 1) + tile, f32),
            vmem((PARTS,) + tile, f32),
            vmem((PARTS,) + tile, f32),
            vmem((SLOTS * CHANNELS, 128), f32),
            vmem(tile, f32), vmem(tile, f32), vmem(tile, f32),
            vmem(tile, f32),
            vmem((GROUP - 1,) + tile, f32),
            vmem(tile, f32),
            vmem((RING - 1,) + tile, f32),
            vmem(tile, f32), vmem(tile, f32), vmem(tile, f32),
            dma((6,)),
            dma((2, PARTS)), dma((2, PARTS)),
            dma((PARTS,)), dma((PARTS,)),
            dma, dma((PARTS,)),
            dma, dma,
            dma, dma, dma, dma,
            dma((2,)), dma((2,)),
            dma((2,)), dma((2,)),
            dma, dma, dma, dma,
            dma((2,)), dma((2,)),
        ],
        compiler_params=pltpu.CompilerParams(
            collective_id=0, has_side_effects=True, vmem_limit_bytes=56 * 1024 * 1024
        ),
    )(
        spectra, counts, band_filter.reshape(1, BINS), jnp.swapaxes(pair_list, 1, 2), live_slots,
        jnp.asarray(turns), jnp.asarray(places),
    )


def solution(mesh):
    placed = (P("win", "pair", None, None), P("win", "pair"), P(), P("pair", None, None), P("pair"))
    return jax.shard_map(
        on_device, mesh=mesh, in_specs=placed, out_specs=P("win", "pair"), check_vma=False
    )
```

time: 95.2 us -> 79.6 us (0.84)
  Pallas kernels: 90.9 us -> 76.4 us
  local copies, waits for them, and re-layouts: 2.77 us -> 1.42 us
    pallas_call x1, Pallas kernels: 90.9 us -> 76.4 us  [on_device(): pl.pallas_call(kernel, out_shape=jax.ShapeDtypeStruct((SHARE, SLOTS * CHA...]
    unnamed x2 -> x1, local copies, waits for them, and re-layouts: 2.77 us -> 1.42 us
where the time goes in v2:
time: 79.6 us; the launch traced here: 79.2 us
  Pallas kernels  76.4 us (96%)
  local copies, waits for them, and re-layouts  1.42 us (2%)
  between operations  1.3 us (2%)
    pallas_call x1, Pallas kernels, on_device(): pl.pallas_call(kernel, out_shape=jax.ShapeDtypeStruct((SHARE, SLOTS * CHA...  76.4 us

profile of v2, /device:TPU:1, one launch (start us, length us, event | category | flops | bytes accessed | tf_op | source)
XLA Modules:
  0.0 79.2 jit_solution(15715444897837689728)
XLA Ops:
  1.3 76.4 %shard_map.73 = f32[32,384]{1,0:T(8,128)} custom-call(f32[2,1,64,4096]{3,2,1,0:T(8,128)} %spectra.1, s32[1,1]{1,0:T(1,128)S(6)} %copy.9.counts_hbm, f32[1,2048]{1,0:T(1,128)} %bitcast.2, s32[1,2,6]{2,1,0:T(2,128)} %bitcast.3, s32[1]{0:T(128)S(6)} %copy.10.live_hbm, f32[2048,128]{1,0:T(8,128)} %constant.4.clone.turns, f32[2048,256]{1,0:T(8,128)} %constant.5.clone.places), custom_call_target="tpu_custom_call" | custom-call | tf_op jit(solution)/shard_map/pallas_call | solution.py:407
  77.7 1.4 %copy.11 = f32[32,384]{1,0:T(8,128)} copy(f32[32,384]{1,0:T(8,128)} %shard_map.73) | data formatting | bytes 98304

commit v3 on v2

--- a/solution.py
+++ b/solution.py
@@ -20,7 +20,12 @@
 PIECE = SHARE * RING
 HALF = PIECE // 2
 LINES = 2 * ROWS
-AHEAD = 3
+AHEAD = 2
+LAST = PARTS - 1
+RUNS = ((0, 1280), (1280, BINS))
+PAIRS = 3
+UNITS = PAIRS + 2
+TAIL = PAIRS - 1
 MESH = pl.DeviceIdType.MESH
 
 
@@ -51,9 +56,10 @@
     counts, pairs, live,
     own, own_level, low, high, turn_table, place_table, table,
     own_stack, own_term, own_got_one, own_pack, own_got_two, own_total, own_low, own_high, own_wide,
-    stack, term, got_one, pack, got_two, total, got_low, chosen,
+    stack, term, got_one, pack, got_two, got_two_low, total, got_low, chosen, level_low, level_high,
     count_own, count_low, count_high, kept, kept_one, kept_part, kept_two, kept_all, kept_low, kept_high,
-    load_sem, halo_send, halo_recv, one_send, one_recv, two_send, two_recv, z_send, z_recv,
+    load_sem, halo_send, halo_recv, one_send, one_recv, two_send, two_recv, two_low_send, two_low_recv, z_send, z_recv,
+    run_send, run_recv, level_send, level_recv,
     own_one_send, own_one_recv, own_two_send, own_two_recv, own_z_send, own_z_recv,
     count_send, count_recv, kept_one_send, kept_one_recv, kept_two_send, kept_two_recv, kept_z_send, kept_z_recv,
 ):
@@ -63,6 +69,9 @@
     member = win % GROUP
     above = (win, (plane + 1) % RING)
     below = (win, (plane + RING - 1) % RING)
+    has_above, has_below = plane < RING - 1, plane > 0
+    sends_up, takes_low = plane < RING - 2, (plane > 0) & (plane < RING - 1)
+    sends_down, takes_high = plane > 0, plane < RING - 1
 
     def in_group(step):
         return (row * GROUP + (member + step) % GROUP, plane)
@@ -70,9 +79,21 @@
     def in_ring(step):
         return (((row + step) % RING) * GROUP + member, plane)
 
+    for ref in (count_low, count_high, kept_low, kept_high):
+        ref[...] = jnp.ones_like(ref)
+    for ref in (own_low, own_high, got_low, level_low, level_high):
+        ref[...] = jnp.zeros_like(ref)
+
     barrier = pltpu.get_barrier_semaphore()
-    for neighbour in (above, below):
-        pl.semaphore_signal(barrier, inc=1, device_id=neighbour, device_id_type=MESH)
+
+    @pl.when(has_above)
+    def _():
+        pl.semaphore_signal(barrier, inc=1, device_id=above, device_id_type=MESH)
+
+    @pl.when(has_below)
+    def _():
+        pl.semaphore_signal(barrier, inc=1, device_id=below, device_id_type=MESH)
+
     for step in range(1, GROUP):
         pl.semaphore_signal(barrier, inc=1, device_id=in_group(step), device_id_type=MESH)
     for step in range(1, RING):
@@ -88,7 +109,7 @@
         load.start()
     count_load.wait()
     count_own[...] = jnp.full((8, 128), counts[0, 0].astype(jnp.float32))
-    pl.semaphore_wait(barrier, 2 + GROUP - 1 + RING - 1)
+    pl.semaphore_wait(barrier, GROUP - 1 + RING - 1 + has_above.astype(jnp.int32) + has_below.astype(jnp.int32))
 
     def remote(source, target, send, recv, device):
         return pltpu.make_async_remote_copy(
@@ -98,25 +119,60 @@
     def whole(ref, send, recv):
         return remote(ref, ref, send, recv, above)
 
+    def both_sides(up, low_ref, down, high_ref, send, recv):
+        return (
+            remote(up, low_ref, send.at[0], recv.at[0], above),
+            remote(down, high_ref, send.at[1], recv.at[1], below),
+        )
+
     def halo(index):
         block = spectra.at[:, 0, pl.ds(pl.multiple_of(index * ROWS, ROWS), ROWS), :]
-        return (
-            remote(block, low.at[index], halo_send.at[0, index], halo_recv.at[0, index], above),
-            remote(block, high.at[index], halo_send.at[1, index], halo_recv.at[1, index], below),
-        )
-
-    def both_sides(source, to_above, to_below, send, recv):
-        return (
-            remote(source, to_above, send.at[0], recv.at[0], above),
-            remote(source, to_below, send.at[1], recv.at[1], below),
-        )
-
-    count_copies = both_sides(count_own, count_low, count_high, count_send, count_recv)
-    for copy in count_copies:
-        copy.start()
+        return both_sides(block, low.at[index], block, high.at[index], halo_send.at[index], halo_recv.at[index])
+
+    def runs(run):
+        copies = []
+        for side in range(2):
+            lanes = pl.ds(side * BINS + RUNS[run][0], RUNS[run][1] - RUNS[run][0])
+            block = spectra.at[:, 0, pl.ds(LAST * ROWS, ROWS), lanes]
+            copies.append(
+                both_sides(
+                    block, low.at[LAST, :, :, lanes], block, high.at[LAST, :, :, lanes],
+                    run_send.at[run, side], run_recv.at[run, side],
+                )
+            )
+        return copies
+
+    def next_halo(index):
+        within = index < LAST
+        begin(halo(lax.rem(index, PARTS)), sends_up & within, sends_down & within)
+        for run in range(len(RUNS)):
+            for copies in runs(run):
+                begin(copies, sends_up & (index == LAST + run), sends_down & (index == LAST + run))
+
+    def begin(copies, up, down):
+        pl.when(up)(copies[0].start)
+        pl.when(down)(copies[1].start)
+
+    def end_send(copies, up, down):
+        pl.when(up)(copies[0].wait_send)
+        pl.when(down)(copies[1].wait_send)
+
+    def end_recv(copies, takes_low, takes_high):
+        pl.when(takes_low)(copies[0].wait_recv)
+        pl.when(takes_high)(copies[1].wait_recv)
+
     for index in range(AHEAD):
-        for copy in halo(index):
-            copy.start()
+        begin(halo(index), sends_up, sends_down)
+    count_copies = both_sides(count_own, count_low, count_own, count_high, count_send, count_recv)
+    begin(count_copies, has_above, has_below)
+
+    @pl.when(jnp.logical_not(takes_low))
+    def _():
+        low[...] = jnp.zeros_like(low)
+
+    @pl.when(jnp.logical_not(takes_high))
+    def _():
+        high[...] = jnp.zeros_like(high)
 
     turn_load.wait()
     place_load.wait()
@@ -187,8 +243,12 @@
 
     own_piece(0)
 
-    for copy in count_copies:
-        copy.wait()
+    last_level = own_level.at[:, pl.ds(LAST * ROWS, ROWS)]
+    level_copies = both_sides(last_level, level_low, last_level, level_high, level_send, level_recv)
+    begin(level_copies, sends_up, sends_down)
+
+    end_recv(count_copies, has_below, has_above)
+    end_send(count_copies, has_above, has_below)
     above_count = count_high[...]
     side = jnp.minimum(mine, above_count)
     across = jnp.minimum(count_low[...], above_count)
@@ -199,15 +259,7 @@
     mask_side = jnp.where(side > 1.5, 1.0, 0.0)
     mask_across = jnp.where(across > 1.5, 1.0, 0.0)
 
-    def correlate(index):
-        for copy in halo(index):
-            copy.wait_recv()
-
-        @pl.when(index + AHEAD < PARTS)
-        def _():
-            for copy in halo(index + AHEAD):
-                copy.start()
-
+    def readers_of(index):
         here = pl.ds(pl.multiple_of(index * ROWS, ROWS), ROWS)
 
         def reader(kind, window):
@@ -216,11 +268,11 @@
             ref = low if kind == 1 else high
             return lambda lanes: ref[index, window, :, lanes]
 
-        readers = {(kind, window): reader(kind, window) for kind in range(3) for window in range(2)}
-        levels = {
-            key: own_level[key[1], here, :] if key[0] == 0 else level(read, ROWS) for key, read in readers.items()
-        }
-        for lane in range(0, BINS, 128):
+        return {(kind, window): reader(kind, window) for kind in range(3) for window in range(2)}
+
+    def products(readers, levels, begin_lane, end_lane, place=0):
+        rows = slice(place * LINES, (place + 1) * LINES)
+        for lane in range(begin_lane, end_lane, 128):
             real, imag = slice(lane, lane + 128), slice(BINS + lane, BINS + lane + 128)
             weight = jnp.broadcast_to(band[:, real], (ROWS, 128))
             re = {key: read(real) * levels[key] for key, read in readers.items()}
@@ -238,25 +290,73 @@
 
             side_re, side_im = cross(0, 2, mask_side)
             across_re, across_im = cross(1, 2, mask_across)
-            stack[:, real] = jnp.concatenate([side_re, across_re], axis=0).astype(jnp.bfloat16)
-            stack[:, imag] = jnp.concatenate([side_im, across_im], axis=0).astype(jnp.bfloat16)
-
-        def piece(step):
-            term[index, step] = lax.dot_general(
-                stack[...],
-                table[(member + step) % GROUP],
-                (((1,), (0,)), ((), ())),
-                preferred_element_type=jnp.float32,
-            )
+            stack[rows, real] = jnp.concatenate([side_re, across_re], axis=0).astype(jnp.bfloat16)
+            stack[rows, imag] = jnp.concatenate([side_im, across_im], axis=0).astype(jnp.bfloat16)
+
+    def times_table(lines, step, rows):
+        return lax.dot_general(
+            stack[0:lines, rows],
+            table[(member + step) % GROUP, rows],
+            (((1,), (0,)), ((), ())),
+            preferred_element_type=jnp.float32,
+        )
+
+    def lines_of(unit):
+        return LINES if isinstance(unit, int) and unit >= PAIRS else 2 * LINES
+
+    def send_piece(unit, step):
+        lines = pl.ds(0, lines_of(unit))
+        remote(
+            term.at[unit, step, lines], got_one.at[unit, step - 1, lines],
+            one_send.at[unit], one_recv.at[unit], in_group(step),
+        ).start()
+
+    def cross_spectra(index, place):
+        end_recv(halo(index), takes_low, takes_high)
+        next_halo(index + AHEAD)
+        here = pl.ds(pl.multiple_of(index * ROWS, ROWS), ROWS)
+        readers = readers_of(index)
+        levels = {
+            key: own_level[key[1], here, :] if key[0] == 0 else level(read, ROWS) for key, read in readers.items()
+        }
+        products(readers, levels, 0, BINS, place)
+
+    def correlate(unit):
+        lines = lines_of(unit)
 
         @pl.loop(1, GROUP)
         def _(step):
-            piece(step)
-            remote(
-                term.at[index, step], got_one.at[index, step - 1], one_send.at[index], one_recv.at[index], in_group(step)
-            ).start()
-
-        piece(0)
+            term[unit, step, 0:lines] = times_table(lines, step, slice(0, 2 * BINS))
+            send_piece(unit, step)
+
+        term[unit, 0, 0:lines] = times_table(lines, 0, slice(0, 2 * BINS))
+
+    def correlate_last():
+        end_recv(level_copies, takes_low, takes_high)
+        end_send(level_copies, sends_up, sends_down)
+        readers = readers_of(LAST)
+        levels = {}
+        for window in range(2):
+            levels[0, window] = own_level[window, LAST * ROWS : PARTS * ROWS, :]
+            levels[1, window] = level_low[window]
+            levels[2, window] = level_high[window]
+        for run, (start, stop) in enumerate(RUNS):
+            for copies in runs(run):
+                end_recv(copies, takes_low, takes_high)
+            products(readers, levels, start, stop)
+            real, imag = slice(start, stop), slice(BINS + start, BINS + stop)
+
+            def piece(step):
+                value = times_table(LINES, step, real) + times_table(LINES, step, imag)
+                term[UNITS - 1, step, 0:LINES] = value if run == 0 else term[UNITS - 1, step, 0:LINES] + value
+
+            @pl.loop(1, GROUP)
+            def _(step):
+                piece(step)
+                if run == len(RUNS) - 1:
+                    send_piece(UNITS - 1, step)
+
+            piece(0)
 
     def packed(groups, chip):
         lane = lax.broadcasted_iota(jnp.int32, groups[0].shape, 1)
@@ -267,47 +367,77 @@
             value = moved if value is None else jnp.where(lane < (place + 1) * SHARE, moved, value)
         return value
 
-    def add_group(index):
-        whole(got_one.at[index], one_send.at[index], one_recv.at[index]).wait_recv()
+    def pieces_of(unit):
+        return got_one.at[unit, :, pl.ds(0, lines_of(unit))]
+
+    def add_group(unit):
+        whole(pieces_of(unit), one_send.at[unit], one_recv.at[unit]).wait_recv()
+        lines = lines_of(unit)
         for half in range(2):
             lanes = slice(half * HALF, (half + 1) * HALF)
-            value = term[index, 0, :, lanes]
+            value = term[unit, 0, 0:lines, lanes]
             for step in range(GROUP - 1):
-                value = value + got_one[index, step, :, lanes]
+                value = value + got_one[unit, step, 0:lines, lanes]
+            groups = [value[start : start + ROWS] for start in range(0, lines, ROWS)]
             for chip in range(RING // 2):
-                pack[index, half * (RING // 2) + chip] = packed([value[:ROWS], value[ROWS:]], chip)
+                pack[unit, half * (RING // 2) + chip] = packed(groups, chip)
         for step in range(1, RING):
             remote(
-                pack.at[index, (row + step) % RING], got_two.at[index, step - 1],
-                two_send, two_recv.at[index], in_ring(step),
+                pack.at[unit, (row + step) % RING], got_two.at[unit, step - 1],
+                two_send, two_recv.at[unit], in_ring(step),
             ).start()
 
-    def add_ring(index):
+    def send_up(index):
+        for step in range(RING):
+            target = (row + step) % RING
+            remote(
+                pack.at[index, target], got_two_low.at[index - TAIL, step], two_low_send, two_low_recv.at[index - TAIL],
+                (target * GROUP + member, plane + 1),
+            ).start()
+
+    def add_group_up(index):
+        add_group(index)
+        pl.when(has_above)(lambda: send_up(index))
+
+    def sum_ring(index):
         whole(got_two.at[index], two_send, two_recv.at[index]).wait_recv()
         value = pack[index, row]
         for step in range(RING - 1):
             value = value + got_two[index, step]
         total[index] = value
-        remote(total.at[index], got_low.at[index], z_send, z_recv, above).start()
-        whole(got_one.at[index], one_send.at[index], one_recv.at[index]).wait_send()
-        for copy in halo(index):
-            copy.wait_send()
-
-    @pl.loop(0, PARTS + 2)
-    def _(turn):
-        @pl.when(turn < PARTS)
+
+    def add_ring(index):
+        sum_ring(index)
+        pl.when(has_above)(remote(total.at[index], got_low.at[index], z_send, z_recv, above).start)
+
+    def sum_low(index):
+        whole(got_two_low.at[index - TAIL], two_low_send, two_low_recv.at[index - TAIL]).wait_recv()
+        value = got_two_low[index - TAIL, 0]
+        for step in range(1, RING):
+            value = value + got_two_low[index - TAIL, step]
+        got_low[index] = value
+
+    def kept_copies():
+        return both_sides(kept_all, kept_low, kept_all, kept_high, kept_z_send, kept_z_recv)
+
+    def own_copies():
+        return both_sides(own_total, own_low, own_total, own_high, own_z_send, own_z_recv)
+
+    @pl.loop(0, PAIRS)
+    def _(unit):
+        cross_spectra(2 * unit, 0)
+        cross_spectra(2 * unit + 1, 1)
+        correlate(unit)
+
+        @pl.when(unit >= 1)
         def _():
-            correlate(turn)
-
-        @pl.when((turn >= 1) & (turn < PARTS + 1))
+            add_group(unit - 1)
+
+        @pl.when(unit >= 2)
         def _():
-            add_group(turn - 1)
-
-        @pl.when(turn >= 2)
-        def _():
-            add_ring(turn - 2)
-
-        @pl.when(turn == 2)
+            add_ring(unit - 2)
+
+        @pl.when(unit == 1)
         def _():
             whole(kept_one, kept_one_send, kept_one_recv).wait()
             value = kept[...]
@@ -332,7 +462,7 @@
                     own_pack.at[(row + step) % RING], own_got_two.at[step - 1], own_two_send, own_two_recv, in_ring(step)
                 ).start()
 
-        @pl.when(turn == 4)
+        @pl.when(unit == 2)
         def _():
             whole(kept_two, kept_two_send, kept_two_recv).wait()
             whole(own_got_two, own_two_send, own_two_recv).wait()
@@ -343,31 +473,32 @@
                 own_value = own_value + own_got_two[step]
             kept_all[...] = value
             own_total[...] = own_value
-            for copy in both_sides(kept_all, kept_low, kept_high, kept_z_send, kept_z_recv):
-                copy.start()
-            for copy in both_sides(own_total, own_low, own_high, own_z_send, own_z_recv):
-                copy.start()
-
-        @pl.when(turn == 6)
-        def _():
-            for copy in both_sides(kept_all, kept_low, kept_high, kept_z_send, kept_z_recv):
-                copy.wait()
-            for copy in both_sides(own_total, own_low, own_high, own_z_send, own_z_recv):
-                copy.wait()
-            for place, source in enumerate((own_low, own_total, own_high)):
-                value = source[...]
-                for block in range(4):
-                    rows = slice(block * 16, (block + 1) * 16)
-                    own_wide[place, rows, :] = pltpu.roll(value, 128 - block * SHARE, axis=1) if block else value
-
+            begin(kept_copies(), has_above, has_below)
+            begin(own_copies(), has_above, has_below)
+
+    cross_spectra(LAST - 1, 0)
+    correlate(PAIRS)
+    correlate_last()
+    add_ring(TAIL - 1)
+    add_group_up(TAIL)
+    add_group_up(PAIRS)
     pairs_load.wait()
     live_load.wait()
-    whole(got_two, two_send, two_recv.at[0]).wait_send()
-    whole(got_low, z_send, z_recv).wait()
+    for copies in (kept_copies(), own_copies()):
+        end_recv(copies, has_below, has_above)
+        end_send(copies, has_above, has_below)
+    for place, source in enumerate((own_low, own_total, own_high)):
+        value = source[...]
+        for block in range(4):
+            rows = slice(block * 16, (block + 1) * 16)
+            own_wide[place, rows, :] = pltpu.roll(value, 128 - block * SHARE, axis=1) if block else value
+    add_group_up(UNITS - 1)
+
     kept_options = [
         kept_low[0:1], kept_low[1:2], kept_all[2:3], kept_all[0:1], kept_all[1:2], kept_high[0:1],
     ]
-    for slot in range(SLOTS):
+
+    def choose(slot, options):
         a, b = pairs[0, 0, slot], pairs[0, 1, slot]
         tests = [
             (a == plane - 1) & (b == plane),
@@ -376,25 +507,58 @@
             (a == plane) & (b == plane + 1),
             (a == plane + 1) & (b == plane + 1),
         ]
-
-        def choose(options):
-            value = options[0]
-            for test, option in zip(tests, options[1:]):
-                value = jnp.where(test, option, value)
-            return value
-
+        value = options[0]
+        for test, option in zip(tests, options[1:]):
+            value = jnp.where(test, option, value)
+        return value
+
+    scales = []
+    for slot in range(SLOTS):
         alive = (slot < live[0]).astype(jnp.float32)
-        scale = jnp.broadcast_to(alive / choose(kept_options), (ROWS, 128))
-        for index in range(PARTS):
+        scales.append(jnp.broadcast_to(alive / choose(slot, kept_options), (ROWS, 128)))
+
+    def fill(unit):
+        for part in range(2 if unit < PAIRS else 1):
+            index = 2 * unit + part if unit < PAIRS else LAST - UNITS + 1 + unit
             rows = slice(index * ROWS, (index + 1) * ROWS)
-            value = choose([
-                own_wide[0, rows], got_low[index], pltpu.roll(total[index], 128 - SHARE, axis=1),
-                own_wide[1, rows], total[index], own_wide[2, rows],
-            ])
-            chosen[slot * CHANNELS + index * ROWS : slot * CHANNELS + (index + 1) * ROWS, :] = value * scale
+            lane = part * 2 * SHARE
+
+            def side(tile):
+                return pltpu.roll(tile, 128 - lane, axis=1) if lane else tile
+
+            options = [
+                own_wide[0, rows], side(got_low[unit]), pltpu.roll(total[unit], 128 - SHARE - lane, axis=1),
+                own_wide[1, rows], side(total[unit]), own_wide[2, rows],
+            ]
+            for slot in range(SLOTS):
+                start = slot * CHANNELS + index * ROWS
+                chosen[start : start + ROWS, :] = choose(slot, options) * scales[slot]
+
+    def settle(unit):
+        sum_ring(unit)
+        pl.when(has_below)(lambda: sum_low(unit))
+        fill(unit)
+
+    early = got_low.at[pl.ds(0, TAIL)]
+    pl.when(has_below)(whole(early, z_send, z_recv).wait_recv)
+    for unit in range(TAIL):
+        fill(unit)
+    pl.when(has_above)(whole(early, z_send, z_recv).wait_send)
+    for unit in range(TAIL, UNITS - 1):
+        settle(unit)
+    for unit in range(UNITS):
+        whole(pieces_of(unit), one_send.at[unit], one_recv.at[unit]).wait_send()
+    for index in range(LAST):
+        end_send(halo(index), sends_up, sends_down)
+    for run in range(len(RUNS)):
+        for copies in runs(run):
+            end_send(copies, sends_up, sends_down)
+    settle(UNITS - 1)
     for block in range(SLOTS * CHANNELS // 128):
         lanes = slice(block * 128, (block + 1) * 128)
         out[:, lanes] = chosen[lanes, :].T[:SHARE]
+    whole(got_two, two_send, two_recv.at[0]).wait_send()
+    pl.when(has_above)(whole(got_two_low, two_low_send, two_low_recv.at[0]).wait_send)
 
 
 def on_device(spectra, counts, band_filter, pair_list, live_slots):
@@ -404,10 +568,11 @@
     tile = (8, 128)
     vmem = pltpu.VMEM
     anywhere = pl.BlockSpec(memory_space=pl.ANY)
+    far = pl.BlockSpec(memory_space=pltpu.HBM)
     return pl.pallas_call(
         kernel,
         out_shape=jax.ShapeDtypeStruct((SHARE, SLOTS * CHANNELS), f32),
-        in_specs=[anywhere, anywhere, pl.BlockSpec(memory_space=vmem), anywhere, anywhere, anywhere, anywhere],
+        in_specs=[anywhere, far, pl.BlockSpec(memory_space=vmem), far, far, anywhere, anywhere],
         out_specs=pl.BlockSpec(memory_space=vmem),
         scratch_shapes=[
             pltpu.SMEM((1, 1), i32), pltpu.SMEM((1, 2, SLOTS), i32), pltpu.SMEM((1,), i32),
@@ -425,14 +590,16 @@
             vmem((RING - 1, 16, 128), f32),
             vmem((16, 128), f32), vmem((16, 128), f32), vmem((16, 128), f32),
             vmem((3, CHANNELS, 128), f32),
-            vmem((LINES, 2 * BINS), bf16),
-            vmem((PARTS, GROUP, LINES, PIECE), f32),
-            vmem((PARTS, GROUP - 1, LINES, PIECE), f32),
-            vmem((PARTS, RING) + tile, f32),
-            vmem((PARTS, RING - 1) + tile, f32),
-            vmem((PARTS,) + tile, f32),
-            vmem((PARTS,) + tile, f32),
+            vmem((2 * LINES, 2 * BINS), bf16),
+            vmem((UNITS, GROUP, 2 * LINES, PIECE), f32),
+            vmem((UNITS, GROUP - 1, 2 * LINES, PIECE), f32),
+            vmem((UNITS, RING) + tile, f32),
+            vmem((UNITS, RING - 1) + tile, f32),
+            vmem((UNITS - TAIL, RING) + tile, f32),
+            vmem((UNITS,) + tile, f32),
+            vmem((UNITS,) + tile, f32),
             vmem((SLOTS * CHANNELS, 128), f32),
+            vmem((2,) + tile, f32), vmem((2,) + tile, f32),
             vmem(tile, f32), vmem(tile, f32), vmem(tile, f32),
             vmem(tile, f32),
             vmem((GROUP - 1,) + tile, f32),
@@ -440,10 +607,13 @@
             vmem((RING - 1,) + tile, f32),
             vmem(tile, f32), vmem(tile, f32), vmem(tile, f32),
             dma((6,)),
-            dma((2, PARTS)), dma((2, PARTS)),
-            dma((PARTS,)), dma((PARTS,)),
-            dma, dma((PARTS,)),
+            dma((PARTS, 2)), dma((PARTS, 2)),
+            dma((UNITS,)), dma((UNITS,)),
+            dma, dma((UNITS,)),
+            dma, dma((UNITS - TAIL,)),
             dma, dma,
+            dma((len(RUNS), 2, 2)), dma((len(RUNS), 2, 2)),
+            dma((2,)), dma((2,)),
             dma, dma, dma, dma,
             dma((2,)), dma((2,)),
             dma((2,)), dma((2,)),

time: 79.6 us -> 75.7 us (0.951)
  Pallas kernels: 76.4 us -> 72.4 us
    pallas_call x1, Pallas kernels: 76.4 us -> 72.4 us  [on_device(): pl.pallas_call(kernel, out_shape=jax.ShapeDtypeStruct((SHARE, SLOTS * CHA...]
where the time goes in v3:
time: 75.7 us; the launch traced here: 75.1 us
  Pallas kernels  72.4 us (96%)
  local copies, waits for them, and re-layouts  1.42 us (2%)
  between operations  1.3 us (2%)
    pallas_call x1, Pallas kernels, on_device(): pl.pallas_call(kernel, out_shape=jax.ShapeDtypeStruct((SHARE, SLOTS * CHA...  72.4 us

profile of v3, /device:TPU:1, one launch (start us, length us, event | category | flops | bytes accessed | tf_op | source)
XLA Modules:
  0.0 75.1 jit_solution(17608964133446840640)
XLA Ops:
  1.3 72.4 %shard_map.73 = f32[32,384]{1,0:T(8,128)} custom-call(f32[2,1,64,4096]{3,2,1,0:T(8,128)} %spectra.1, s32[1,1]{1,0:T(1,128)S(6)} %copy.9.counts_hbm, f32[1,2048]{1,0:T(1,128)} %bitcast.2, s32[1,2,6]{2,1,0:T(2,128)} %bitcast.3, s32[1]{0:T(128)S(6)} %copy.10.live_hbm, f32[2048,128]{1,0:T(8,128)} %constant.4.clone.turns, f32[2048,256]{1,0:T(8,128)} %constant.5.clone.places), custom_call_target="tpu_custom_call" | custom-call | tf_op jit(solution)/shard_map/pallas_call | solution.py:572
  73.7 1.4 %copy.11 = f32[32,384]{1,0:T(8,128)} copy(f32[32,384]{1,0:T(8,128)} %shard_map.73) | data formatting | bytes 98304

commit v4 on v3

--- a/solution.py
+++ b/solution.py
@@ -26,7 +26,12 @@
 PAIRS = 3
 UNITS = PAIRS + 2
 TAIL = PAIRS - 1
+FAR_FIRST = (4, 3, 5, 2, 6, 1, 7)
 MESH = pl.DeviceIdType.MESH
+
+
+def far_first(count):
+    return GROUP // 2 + (count // 2) * ((count % 2) * 2 - 1)
 
 
 def twiddles():
@@ -325,7 +330,8 @@
         lines = lines_of(unit)
 
         @pl.loop(1, GROUP)
-        def _(step):
+        def _(count):
+            step = far_first(count)
             term[unit, step, 0:lines] = times_table(lines, step, slice(0, 2 * BINS))
             send_piece(unit, step)
 
@@ -351,7 +357,8 @@
                 term[UNITS - 1, step, 0:LINES] = value if run == 0 else term[UNITS - 1, step, 0:LINES] + value
 
             @pl.loop(1, GROUP)
-            def _(step):
+            def _(count):
+                step = far_first(count)
                 piece(step)
                 if run == len(RUNS) - 1:
                     send_piece(UNITS - 1, step)
@@ -370,7 +377,7 @@
     def pieces_of(unit):
         return got_one.at[unit, :, pl.ds(0, lines_of(unit))]
 
-    def add_group(unit):
+    def add_group(unit, up=False):
         whole(pieces_of(unit), one_send.at[unit], one_recv.at[unit]).wait_recv()
         lines = lines_of(unit)
         for half in range(2):
@@ -381,23 +388,22 @@
             groups = [value[start : start + ROWS] for start in range(0, lines, ROWS)]
             for chip in range(RING // 2):
                 pack[unit, half * (RING // 2) + chip] = packed(groups, chip)
-        for step in range(1, RING):
+        for step in FAR_FIRST:
+            if up:
+                pl.when(has_above)(piece_up(unit, step).start)
             remote(
                 pack.at[unit, (row + step) % RING], got_two.at[unit, step - 1],
                 two_send, two_recv.at[unit], in_ring(step),
             ).start()
-
-    def send_up(index):
-        for step in range(RING):
-            target = (row + step) % RING
-            remote(
-                pack.at[index, target], got_two_low.at[index - TAIL, step], two_low_send, two_low_recv.at[index - TAIL],
-                (target * GROUP + member, plane + 1),
-            ).start()
-
-    def add_group_up(index):
-        add_group(index)
-        pl.when(has_above)(lambda: send_up(index))
+        if up:
+            pl.when(has_above)(piece_up(unit, 0).start)
+
+    def piece_up(unit, step):
+        target = (row + step) % RING
+        return remote(
+            pack.at[unit, target], got_two_low.at[unit - TAIL, step], two_low_send, two_low_recv.at[unit - TAIL],
+            (target * GROUP + member, plane + 1),
+        )
 
     def sum_ring(index):
         whole(got_two.at[index], two_send, two_recv.at[index]).wait_recv()
@@ -480,8 +486,8 @@
     correlate(PAIRS)
     correlate_last()
     add_ring(TAIL - 1)
-    add_group_up(TAIL)
-    add_group_up(PAIRS)
+    add_group(TAIL, up=True)
+    add_group(PAIRS, up=True)
     pairs_load.wait()
     live_load.wait()
     for copies in (kept_copies(), own_copies()):
@@ -492,7 +498,7 @@
         for block in range(4):
             rows = slice(block * 16, (block + 1) * 16)
             own_wide[place, rows, :] = pltpu.roll(value, 128 - block * SHARE, axis=1) if block else value
-    add_group_up(UNITS - 1)
+    add_group(UNITS - 1, up=True)
 
     kept_options = [
         kept_low[0:1], kept_low[1:2], kept_all[2:3], kept_all[0:1], kept_all[1:2], kept_high[0:1],

time: 75.7 us -> 75.2 us (level)
  no operation moved by 1% of the time
where the time goes in v4:
time: 75.2 us; the launch traced here: 74.6 us
  Pallas kernels  71.9 us (96%)
  local copies, waits for them, and re-layouts  1.42 us (2%)
  between operations  1.3 us (2%)
    pallas_call x1, Pallas kernels, on_device(): pl.pallas_call(kernel, out_shape=jax.ShapeDtypeStruct((SHARE, SLOTS * CHA...  71.9 us

profile of v4, /device:TPU:1, one launch (start us, length us, event | category | flops | bytes accessed | tf_op | source)
XLA Modules:
  0.0 74.6 jit_solution(13034756601147825445)
XLA Ops:
  1.3 71.9 %shard_map.73 = f32[32,384]{1,0:T(8,128)} custom-call(f32[2,1,64,4096]{3,2,1,0:T(8,128)} %spectra.1, s32[1,1]{1,0:T(1,128)S(6)} %copy.9.counts_hbm, f32[1,2048]{1,0:T(1,128)} %bitcast.2, s32[1,2,6]{2,1,0:T(2,128)} %bitcast.3, s32[1]{0:T(128)S(6)} %copy.10.live_hbm, f32[2048,128]{1,0:T(8,128)} %constant.4.clone.turns, f32[2048,256]{1,0:T(8,128)} %constant.5.clone.places), custom_call_target="tpu_custom_call" | custom-call | tf_op jit(solution)/shard_map/pallas_call | solution.py:578
  73.2 1.4 %copy.11 = f32[32,384]{1,0:T(8,128)} copy(f32[32,384]{1,0:T(8,128)} %shard_map.73) | data formatting | bytes 98304

commit v5 on v4

--- a/solution.py
+++ b/solution.py
@@ -488,6 +488,7 @@
     add_ring(TAIL - 1)
     add_group(TAIL, up=True)
     add_group(PAIRS, up=True)
+    add_group(UNITS - 1, up=True)
     pairs_load.wait()
     live_load.wait()
     for copies in (kept_copies(), own_copies()):
@@ -498,7 +499,6 @@
         for block in range(4):
             rows = slice(block * 16, (block + 1) * 16)
             own_wide[place, rows, :] = pltpu.roll(value, 128 - block * SHARE, axis=1) if block else value
-    add_group(UNITS - 1, up=True)
 
     kept_options = [
         kept_low[0:1], kept_low[1:2], kept_all[2:3], kept_all[0:1], kept_all[1:2], kept_high[0:1],

time: 75.2 us -> 75.2 us (level)
  no operation moved by 1% of the time
where the time goes in v5:
time: 75.2 us; the launch traced here: 74.6 us
  Pallas kernels  71.9 us (96%)
  local copies, waits for them, and re-layouts  1.42 us (2%)
  between operations  1.3 us (2%)
    pallas_call x1, Pallas kernels, on_device(): pl.pallas_call(kernel, out_shape=jax.ShapeDtypeStruct((SHARE, SLOTS * CHA...  71.9 us

profile of v5, /device:TPU:1, one launch (start us, length us, event | category | flops | bytes accessed | tf_op | source)
XLA Modules:
  0.0 74.6 jit_solution(4836907248736001488)
XLA Ops:
  1.3 71.9 %shard_map.73 = f32[32,384]{1,0:T(8,128)} custom-call(f32[2,1,64,4096]{3,2,1,0:T(8,128)} %spectra.1, s32[1,1]{1,0:T(1,128)S(6)} %copy.9.counts_hbm, f32[1,2048]{1,0:T(1,128)} %bitcast.2, s32[1,2,6]{2,1,0:T(2,128)} %bitcast.3, s32[1]{0:T(128)S(6)} %copy.10.live_hbm, f32[2048,128]{1,0:T(8,128)} %constant.4.clone.turns, f32[2048,256]{1,0:T(8,128)} %constant.5.clone.places), custom_call_target="tpu_custom_call" | custom-call | tf_op jit(solution)/shard_map/pallas_call | solution.py:578
  73.2 1.4 %copy.11 = f32[32,384]{1,0:T(8,128)} copy(f32[32,384]{1,0:T(8,128)} %shard_map.73) | data formatting | bytes 98304
